TPU v7x, 512 devices: a whole 4x4x16 slice. The times are simulated.
512 devices in a mesh: zonal: 64 (over x_hi, z, core), merid: 8 (over y, x_lo).
Axes of the slice: x: 4 (x_hi: 2, x_lo: 2; x = x_hi * 2 + x_lo), y: 4, z: 16, core: 2. Of those that a mesh axis runs over, the one named last changes fastest.
Arguments:
- zonal_current_speed: float32 [3, 1024, 8192], P(None, 'merid', 'zonal'), may hold values from -6 to 6
- meridional_current_speed: float32 [3, 1024, 8192], P(None, 'merid', 'zonal'), may hold values from -6 to 6
- thermal_anomaly: float32 [3, 1024, 8192], P(None, 'merid', 'zonal'), may hold values from -6 to 6
- saltiness_anomaly: float32 [3, 1024, 8192], P(None, 'merid', 'zonal'), may hold values from -6 to 6
- zonal_cell_width: float32 [1024, 8192], P('merid', 'zonal'), may hold values from 0.7 to 1.4
- meridional_cell_width: float32 [1024, 8192], P('merid', 'zonal'), may hold values from 0.7 to 1.4
- planetary_rotation_factor: float32 [1024, 8192], P('merid', 'zonal'), may hold values from -1.5 to 1.5
- cell_wet_indicator: int32 [3, 1024, 8192], P(None, 'merid', 'zonal'), may hold values from 0 to 1, as said below
- zonal_edge_wet_indicator: int32 [3, 1024, 8192], P(None, 'merid', 'zonal'), may hold values from 0 to 1, as said below
- meridional_edge_wet_indicator: int32 [3, 1024, 8192], P(None, 'merid', 'zonal'), may hold values from 0 to 1, as said below
- hinge_displacement: int32 [4], replicated, may hold values from 0 to 1
Outputs:
- zonal_out: float32 [3, 1024, 8192], P(None, 'merid', 'zonal')
- merid_out: float32 [3, 1024, 8192], P(None, 'merid', 'zonal')
- temperature_out: float32 [3, 1024, 8192], P(None, 'merid', 'zonal')
- salinity_out: float32 [3, 1024, 8192], P(None, 'merid', 'zonal')
Inputs may be any that keep to these rules, and one draw needn't show every extreme that they name: `cell_wet_indicator`: 1 where a cell is sea at that level; a column that is sea at a level is sea at every level above it. `zonal_edge_wet_indicator`: 1 where the cell and its eastern neighbour (periodic) are both sea. `meridional_edge_wet_indicator`: 1 where the cell and its northern neighbour are both sea; on the northernmost row, where the cell is sea.
All inputs are finite; a program needn't handle non-finite values.
Results may differ from a plain program's by a relative error of at most 0.00002.
Values sent between devices are 32-bit elements; how exact they have to be, the bound alone decides.
A program may use at most 128 MiB of HBM per device.

v0:
```python
import jax
import jax.numpy as jnp
from jax import lax
from jax.sharding import PartitionSpec as P

STEPS = 4


TIME_STEP = 0.25
VISCOSITY = 0.25
DIFFUSIVITY = 0.25


def extended(cells, sides, width, closed):
    for axis, dim in sides:
        count = lax.axis_size(axis)
        ends = count if closed else count - 1
        head = lax.slice_in_dim(cells, 0, width, axis=dim)
        tail = lax.slice_in_dim(cells, cells.shape[dim] - width, cells.shape[dim], axis=dim)
        cells = jnp.concatenate(
            [
                lax.ppermute(tail, axis, [(i, (i + 1) % count) for i in range(ends)]),
                cells,
                lax.ppermute(head, axis, [((i + 1) % count, i) for i in range(ends)]),
            ],
            axis=dim,
        )
    return cells


def passed_along(block, axis, distance):
    devices = range(lax.axis_size(axis))
    route = [((i - distance) % len(devices), i) for i in devices]
    return lax.ppermute(block, axis, route)


def shifted(block, axis, distance):
    devices = range(lax.axis_size(axis))
    route = [(i - distance, i) for i in devices if i - distance in devices]
    return lax.ppermute(block, axis, route)


def water_column_weight(thermal_anomaly, saltiness_anomaly):
    gravity_density_term = 0.5 * thermal_anomaly - 0.4 * saltiness_anomaly
    return jnp.cumsum(gravity_density_term, axis=0) - 0.5 * gravity_density_term


def momentum_fluxes(
    evolving_state_quantities,
    eastern,
    western,
    northern,
    southern,
    zonal_cell_width,
    meridional_cell_width,
    planetary_rotation_factor,
    zonal_float,
    merid_float,
):
    zonal_vel = evolving_state_quantities[0]
    merid_vel = evolving_state_quantities[1]
    pressure_here = water_column_weight(evolving_state_quantities[2], evolving_state_quantities[3])

    def laplace(which_field):
        middle = evolving_state_quantities[which_field]
        return (
            eastern[which_field] - 2.0 * middle + western[which_field]
        ) / zonal_cell_width**2 + (
            northern[which_field] - 2.0 * middle + southern[which_field]
        ) / meridional_cell_width**2

    zonal_new = zonal_float * (
        zonal_vel
        + TIME_STEP
        * (
            planetary_rotation_factor * 0.5 * (merid_vel + southern[1])
            - (water_column_weight(eastern[2], eastern[3]) - pressure_here) / zonal_cell_width
            + VISCOSITY * laplace(0)
        )
    )
    merid_new = merid_float * (
        merid_vel
        + TIME_STEP
        * (
            -planetary_rotation_factor * 0.5 * (zonal_vel + western[0])
            - (water_column_weight(northern[2], northern[3]) - pressure_here)
            / meridional_cell_width
            + VISCOSITY * laplace(1)
        )
    )
    tracers = evolving_state_quantities[2:]
    flux_east = (
        zonal_float
        * meridional_cell_width
        * (
            zonal_new * 0.5 * (tracers + eastern[2:])
            - DIFFUSIVITY * (eastern[2:] - tracers) / zonal_cell_width
        )
    )
    flux_north = (
        merid_float
        * zonal_cell_width
        * (
            merid_new * 0.5 * (tracers + northern[2:])
            - DIFFUSIVITY * (northern[2:] - tracers) / meridional_cell_width
        )
    )
    return (zonal_new, merid_new, flux_east, flux_north)


def fold_partner(source_rows):
    gathered = lax.all_gather(source_rows[None], "zonal", axis=0, tiled=True)
    mirror = lax.axis_size("zonal") - 1 - lax.axis_index("zonal")
    return lax.dynamic_index_in_dim(gathered, mirror, 0, keepdims=False)


def per_device(
    zonal_current_speed,
    meridional_current_speed,
    thermal_anomaly,
    saltiness_anomaly,
    zonal_cell_width,
    meridional_cell_width,
    planetary_rotation_factor,
    cell_wet_indicator,
    zonal_edge_wet_indicator,
    meridional_edge_wet_indicator,
    hinge_displacement,
):
    cell_float = cell_wet_indicator.astype(jnp.float32)
    zonal_float = zonal_edge_wet_indicator.astype(jnp.float32)
    merid_float = meridional_edge_wet_indicator.astype(jnp.float32)
    scalar_wet_indicators = jnp.stack([zonal_float, merid_float, cell_float, cell_float])
    evolving_state_quantities = (
        jnp.stack(
            [zonal_current_speed, meridional_current_speed, thermal_anomaly, saltiness_anomaly]
        )
        * scalar_wet_indicators
    )
    height = evolving_state_quantities.shape[2]
    breadth = evolving_state_quantities.shape[3]
    offsets = hinge_displacement.reshape(4, 1, 1)
    field_signs = jnp.array([-1.0, -1.0, 1.0, 1.0], jnp.float32).reshape(4, 1, 1)
    top_row = lax.axis_index("merid") == lax.axis_size("merid") - 1
    for substep in range(STEPS):
        zonal_pad = extended(evolving_state_quantities, (("zonal", 3),), 1, True)
        merid_pad = extended(evolving_state_quantities, (("merid", 2),), 1, False)
        source_rows = jnp.where(
            offsets == 0, zonal_pad[:, :, height - 1, :], zonal_pad[:, :, height - 2, :]
        )
        partner = fold_partner(source_rows)
        flipped = partner[..., ::-1]
        ghost_row = jnp.where(offsets == 1, flipped[..., 0:breadth], flipped[..., 1 : breadth + 1])
        ghost_row = field_signs * ghost_row
        upper = jnp.where(top_row, ghost_row, merid_pad[:, :, height + 1, :])
        northern = jnp.concatenate(
            [merid_pad[:, :, 2 : height + 1, :], upper[:, :, None, :]], axis=2
        )
        southern = merid_pad[:, :, 0:height, :]
        eastern = zonal_pad[..., 2:]
        western = zonal_pad[..., :-2]
        zonal_new, merid_new, flux_east, flux_north = momentum_fluxes(
            evolving_state_quantities,
            eastern,
            western,
            northern,
            southern,
            zonal_cell_width,
            meridional_cell_width,
            planetary_rotation_factor,
            zonal_float,
            merid_float,
        )
        west_column = passed_along(flux_east[..., breadth - 1 :], "zonal", 1)
        flux_west = jnp.concatenate([west_column, flux_east[..., : breadth - 1]], axis=3)
        south_strip = shifted(flux_north[:, :, height - 1 :, :], "merid", 1)
        flux_south = jnp.concatenate([south_strip, flux_north[:, :, : height - 1, :]], axis=2)
        tracers = cell_float * (
            evolving_state_quantities[2:]
            - TIME_STEP
            * (flux_east - flux_west + flux_north - flux_south)
            / (zonal_cell_width * meridional_cell_width)
        )
        evolving_state_quantities = jnp.concatenate(
            [zonal_new[None], merid_new[None], tracers], axis=0
        )
    return (
        evolving_state_quantities[0],
        evolving_state_quantities[1],
        evolving_state_quantities[2],
        evolving_state_quantities[3],
    )


def solution(mesh):
    placed = (
        P(None, "merid", "zonal"),
        P(None, "merid", "zonal"),
        P(None, "merid", "zonal"),
        P(None, "merid", "zonal"),
        P("merid", "zonal"),
        P("merid", "zonal"),
        P("merid", "zonal"),
        P(None, "merid", "zonal"),
        P(None, "merid", "zonal"),
        P(None, "merid", "zonal"),
        P(),
    )
    return jax.shard_map(
        per_device,
        mesh=mesh,
        in_specs=placed,
        out_specs=(
            P(None, "merid", "zonal"),
            P(None, "merid", "zonal"),
            P(None, "merid", "zonal"),
            P(None, "merid", "zonal"),
        ),
        check_vma=False,
    )
```

profile of v0, /device:TPU:18, one launch (start us, length us, event | category | flops | bytes accessed | tf_op | source)
XLA Modules:
  0.0 442.6 jit_solution(7539267975058116440)
XLA Ops:
  0.7 1.7 fusion.293
  2.4 0.9 copy-done.52
  4.2 12.4 %collective-permute-start.1 = (f32[4,3,128,1]{2,0,3,1:T(4,128)S(1)}, f32[4,3,128,1]{2,0,3,1:T(4,128)S(1)}, u32[]{:S(2)}, u32[]{:S(2)}) collective-permute-start(f32[4,3,128,1]{2,0,3,1:T(4,128)S(1)} %copy.488), channel_id=1, source_target_pairs={{8,0},{16,8},{24,16},{32,24},{40,32},{48,40},{56,48},{64,56},{72,6... | collective-permute-start | bytes 18440 | tf_op jit(solution)/shard_map/ppermute | solution.py:24
  16.9 1.9 collective-permute-start.2
  18.8 0.6 fusion.292
  19.4 3.3 collective-permute-start.3
  22.8 3.5 collective-permute-start
  26.3 0.7 reduce-window_subtract_fusion.10
  27.0 0.7 convert_multiply_fusion
  27.9 0.7 fusion.294
  28.7 0.6 negate_multiply_fusion
  29.8 1.0 copy.491
  30.9 74.4 %all_gather.12 = f32[64,4,3,130]{3,1,2,0:T(4,128)S(1)} all-gather(f32[1,4,3,130]{3,1,2,0:T(4,128)S(1)} %copy.494), channel_id=1, replica_groups=mesh['zonal'=64,'merid'=8] {'zonal'}, dimensions={0}, use_global_device_ids=true | all-gather | bytes 405600 | tf_op jit(solution)/shard_map/all_gather | solution.py:112
  105.7 0.7 copy-done.57
  106.3 0.8 fusion.251
  107.2 1.8 broadcast_multiply_fusion.7
  109.1 1.2 broadcast_multiply_fusion.6
  110.3 0.3 subtract_multiply_fusion.7
  110.8 2.3 collective-permute-start.4
  113.1 3.7 collective-permute-start.5
  116.8 6.7 %collective-permute-done.4 = f32[2,3,128,1]{3,2,1,0:T(8,128)S(1)} collective-permute-done((f32[2,3,128,1]{3,2,1,0:T(8,128)S(1)}, f32[2,3,128,1]{3,2,1,0:T(8,128)S(1)}, u32[]{:S(2)}, u32[]{:S(2)}) %collective-permute-start.4) | collective-permute-done | bytes 3104 | tf_op jit(solution)/shard_map/ppermute | solution.py:34
  123.8 0.7 reduce-window_subtract_fusion.7
  125.1 1.9 collective-permute-start.7
  127.3 2.4 collective-permute-start.8
  129.7 0.6 pad_maximum_fusion.55
  130.4 2.5 collective-permute-start.9
  132.9 4.2 collective-permute-start.6
  138.2 0.8 copy-done
  139.1 73.6 %all_gather.13 = f32[64,4,3,130]{3,1,2,0:T(4,128)S(1)} all-gather(f32[1,4,3,130]{3,1,2,0:T(4,128)S(1)} %copy.503), channel_id=1, replica_groups=mesh['zonal'=64,'merid'=8] {'zonal'}, dimensions={0}, use_global_device_ids=true | all-gather | bytes 405600 | tf_op jit(solution)/shard_map/all_gather | solution.py:112
  212.9 0.8 fusion.250
  213.8 1.4 broadcast_multiply_fusion.4
  215.3 0.7 broadcast_multiply_fusion.5
  216.3 0.3 subtract_multiply_fusion.5
  216.8 2.3 collective-permute-start.10
  219.1 3.4 collective-permute-start.11
  222.5 7.0 %collective-permute-done.10 = f32[2,3,128,1]{3,2,1,0:T(8,128)S(1)} collective-permute-done((f32[2,3,128,1]{3,2,1,0:T(8,128)S(1)}, f32[2,3,128,1]{3,2,1,0:T(8,128)S(1)}, u32[]{:S(2)}, u32[]{:S(2)}) %collective-permute-start.10) | collective-permute-done | bytes 3104 | tf_op jit(solution)/shard_map/ppermute | solution.py:34
  229.8 0.7 reduce-window_subtract_fusion.4
  231.1 1.9 collective-permute-start.13
  233.3 2.4 collective-permute-start.14
  235.8 1.9 collective-permute-start.15
  237.7 4.8 %collective-permute-start.12 = (f32[4,3,1,128]{3,2,1,0:T(1,128)S(1)}, f32[4,3,1,128]{3,2,1,0:T(1,128)S(1)}, u32[]{:S(2)}, u32[]{:S(2)}) collective-permute-start(f32[4,3,1,128]{3,2,1,0:T(1,128)S(1)} %get-tuple-element.19), channel_id=1, source_target_pairs={{0,1},{1,2},{2,3},{3,4},{4,5},{5,6},{6,7},{8,9},{9,10},{10,11},{11... | collective-permute-start | bytes 18440 | tf_op jit(solution)/shard_map/ppermute | solution.py:22
  243.7 73.4 %all_gather.14 = f32[64,4,3,130]{3,1,2,0:T(4,128)S(1)} all-gather(f32[1,4,3,130]{3,1,2,0:T(4,128)S(1)} %copy.512), channel_id=1, replica_groups=mesh['zonal'=64,'merid'=8] {'zonal'}, dimensions={0}, use_global_device_ids=true | all-gather | bytes 405600 | tf_op jit(solution)/shard_map/all_gather | solution.py:112
  317.5 1.5 broadcast_multiply_fusion.2
  319.1 0.7 broadcast_multiply_fusion.3
  320.1 0.3 subtract_multiply_fusion.3
  320.6 2.4 collective-permute-start.16
  323.1 2.5 collective-permute-start.17
  325.6 7.8 %collective-permute-done.16 = f32[2,3,128,1]{3,2,1,0:T(8,128)S(1)} collective-permute-done((f32[2,3,128,1]{3,2,1,0:T(8,128)S(1)}, f32[2,3,128,1]{3,2,1,0:T(8,128)S(1)}, u32[]{:S(2)}, u32[]{:S(2)}) %collective-permute-start.16) | collective-permute-done | bytes 3104 | tf_op jit(solution)/shard_map/ppermute | solution.py:34
  333.7 0.7 reduce-window_subtract_fusion.1
  335.0 1.9 collective-permute-start.19
  337.2 2.4 collective-permute-start.20
  339.6 0.6 pad_maximum_fusion.51
  340.3 1.9 collective-permute-start.21
  342.2 4.8 %collective-permute-start.18 = (f32[4,3,1,128]{3,2,1,0:T(1,128)}, f32[4,3,1,128]{3,2,1,0:T(1,128)}, u32[]{:S(2)}, u32[]{:S(2)}) collective-permute-start(f32[4,3,1,128]{3,2,1,0:T(1,128)} %get-tuple-element.15), channel_id=1, source_target_pairs={{0,1},{1,2},{2,3},{3,4},{4,5},{5,6},{6,7},{8,9},{9,10},{10,11},{11... | collective-permute-start | bytes 18440 | tf_op jit(solution)/shard_map/ppermute | solution.py:22
  348.2 73.6 %all_gather.15 = f32[64,4,3,130]{3,1,2,0:T(4,128)S(1)} all-gather(f32[1,4,3,130]{3,1,2,0:T(4,128)S(1)} %copy.521), channel_id=1, replica_groups=mesh['zonal'=64,'merid'=8] {'zonal'}, dimensions={0}, use_global_device_ids=true | all-gather | bytes 405600 | tf_op jit(solution)/shard_map/all_gather | solution.py:112
  421.7 0.7 fusion.295
  422.5 0.8 slice.574
  423.3 0.8 fusion.248
  424.2 2.1 broadcast_multiply_fusion
  426.3 2.1 broadcast_multiply_fusion.1
  428.9 2.3 collective-permute-start.22
  431.1 2.3 collective-permute-start.23
  433.4 8.1 %collective-permute-done.22 = f32[2,3,128,1]{3,2,1,0:T(8,128)S(1)} collective-permute-done((f32[2,3,128,1]{3,2,1,0:T(8,128)S(1)}, f32[2,3,128,1]{3,2,1,0:T(8,128)S(1)}, u32[]{:S(2)}, u32[]{:S(2)}) %collective-permute-start.22) | collective-permute-done | bytes 3104 | tf_op jit(solution)/shard_map/ppermute | solution.py:34
  441.8 0.8 slice_bitcast_fusion
  (215 shorter events, 11.9 us)
Async XLA Ops:
  0.6 1.7 copy-start.35
  0.6 1.7 copy-start.2
  4.2 25.3 %collective-permute-start.1 = (f32[4,3,128,1]{2,0,3,1:T(4,128)S(1)}, f32[4,3,128,1]{2,0,3,1:T(4,128)S(1)}, u32[]{:S(2)}, u32[]{:S(2)}) collective-permute-start(f32[4,3,128,1]{2,0,3,1:T(4,128)S(1)} %copy.488), channel_id=1, source_target_pairs={{8,0},{16,8},{24,16},{32,24},{40,32},{48,40},{56,48},{64,56},{72,6... | collective-permute-start | bytes 18440 | tf_op jit(solution)/shard_map/ppermute | solution.py:24
  16.9 12.9 %collective-permute-start.2 = (f32[4,3,128,1]{2,0,3,1:T(4,128)S(1)}, f32[4,3,128,1]{2,0,3,1:T(4,128)}, u32[]{:S(2)}, u32[]{:S(2)}) collective-permute-start(f32[4,3,128,1]{2,0,3,1:T(4,128)S(1)} %copy.490), channel_id=1, source_target_pairs={{0,8},{8,16},{16,24},{24,32},{32,40},{40,48},{48,56},{56,64},{64,7... | collective-permute-start | bytes 18440 | tf_op jit(solution)/shard_map/ppermute | solution.py:22
  19.4 86.2 %collective-permute-start.3 = (f32[4,3,1,128]{3,2,1,0:T(1,128)}, f32[4,3,1,128]{3,2,1,0:T(1,128)}, u32[]{:S(2)}, u32[]{:S(2)}) collective-permute-start(f32[4,3,1,128]{3,2,1,0:T(1,128)} %get-tuple-element.28), channel_id=1, source_target_pairs={{1,0},{2,1},{3,2},{4,3},{5,4},{6,5},{7,6},{9,8},{10,9},{11,10},{12... | collective-permute-start | bytes 18440 | tf_op jit(solution)/shard_map/ppermute | solution.py:24
  22.8 4.3 copy-start.11
  22.8 84.3 %collective-permute-start = (f32[4,3,1,128]{3,2,1,0:T(1,128)}, f32[4,3,1,128]{3,2,1,0:T(1,128)S(1)}, u32[]{:S(2)}, u32[]{:S(2)}) collective-permute-start(f32[4,3,1,128]{3,2,1,0:T(1,128)} %get-tuple-element.29), channel_id=1, source_target_pairs={{0,1},{1,2},{2,3},{3,4},{4,5},{5,6},{6,7},{8,9},{9,10},{10,11},{11... | collective-permute-start | bytes 18440 | tf_op jit(solution)/shard_map/ppermute | solution.py:22
  28.7 78.4 %copy-start.16 = (f32[128,128]{1,0:T(8,128)}, f32[128,128]{1,0:T(8,128)S(1)}, u32[]{:S(2)}) copy-start(f32[128,128]{1,0:T(8,128)S(1)} %get-tuple-element.42) | copy-start | bytes 196612
  29.4 288.0 %copy-start.58 = (pred[4]{0:T(512)(128)(4,1)}, pred[4]{0:T(512)(128)(4,1)S(1)}, u32[]{:S(2)}) copy-start(pred[4]{0:T(512)(128)(4,1)S(1)} %get-tuple-element.54) | copy-start | bytes 16
  107.1 1.9 copy-start.3
  107.1 1.9 copy-start.7
  107.1 1.9 copy-start.20
  107.2 1.9 copy-start.39
  107.2 1.9 copy-start.47
  110.6 12.9 %copy-start.32 = (f32[3,128,128]{2,1,0:T(8,128)S(1)}, f32[3,128,128]{2,1,0:T(8,128)}, u32[]{:S(2)}) copy-start(f32[3,128,128]{2,1,0:T(8,128)} %get-tuple-element.38) | copy-start | bytes 589828
  110.6 12.9 %copy-start.49 = (f32[128,128]{1,0:T(8,128)S(1)}, f32[128,128]{1,0:T(8,128)}, u32[]{:S(2)}) copy-start(f32[128,128]{1,0:T(8,128)} %get-tuple-element.41) | copy-start | bytes 196612
  110.8 12.7 %collective-permute-start.4 = (f32[2,3,128,1]{3,2,1,0:T(8,128)S(1)}, f32[2,3,128,1]{3,2,1,0:T(8,128)S(1)}, u32[]{:S(2)}, u32[]{:S(2)}) collective-permute-start(f32[2,3,128,1]{3,2,1,0:T(8,128)S(1)} %slice.611), channel_id=1, source_target_pairs={{504,0},{0,8},{8,16},{16,24},{24,32},{32,40},{40,48},{48,56},{56,6... | collective-permute-start | bytes 9224 | tf_op jit(solution)/shard_map/ppermute | solution.py:34
  113.1 10.4 %collective-permute-start.5 = (f32[2,3,1,128]{3,2,1,0:T(1,128)S(1)}, f32[2,3,1,128]{3,2,1,0:T(1,128)S(1)}, u32[]{:S(2)}, u32[]{:S(2)}) collective-permute-start(f32[2,3,1,128]{3,2,1,0:T(1,128)S(1)} %slice.613), channel_id=1, source_target_pairs={{0,1},{1,2},{2,3},{3,4},{4,5},{5,6},{6,7},{8,9},{9,10},{10,11},{11... | collective-permute-start | bytes 9224 | tf_op jit(solution)/shard_map/ppermute | solution.py:40
  125.1 12.0 %collective-permute-start.7 = (f32[4,3,128,1]{2,0,3,1:T(4,128)S(1)}, f32[4,3,128,1]{2,0,3,1:T(4,128)S(1)}, u32[]{:S(2)}, u32[]{:S(2)}) collective-permute-start(f32[4,3,128,1]{2,0,3,1:T(4,128)S(1)} %copy.497), channel_id=1, source_target_pairs={{8,0},{16,8},{24,16},{32,24},{40,32},{48,40},{56,48},{64,56},{72,6... | collective-permute-start | bytes 18440 | tf_op jit(solution)/shard_map/ppermute | solution.py:24
  127.3 10.2 %collective-permute-start.8 = (f32[4,3,128,1]{2,0,3,1:T(4,128)S(1)}, f32[4,3,128,1]{2,0,3,1:T(4,128)S(1)}, u32[]{:S(2)}, u32[]{:S(2)}) collective-permute-start(f32[4,3,128,1]{2,0,3,1:T(4,128)S(1)} %copy.499), channel_id=1, source_target_pairs={{0,8},{8,16},{16,24},{24,32},{32,40},{40,48},{48,56},{56,64},{64,7... | collective-permute-start | bytes 18440 | tf_op jit(solution)/shard_map/ppermute | solution.py:22
  130.4 82.5 %collective-permute-start.9 = (f32[4,3,1,128]{3,2,1,0:T(1,128)}, f32[4,3,1,128]{3,2,1,0:T(1,128)}, u32[]{:S(2)}, u32[]{:S(2)}) collective-permute-start(f32[4,3,1,128]{3,2,1,0:T(1,128)} %get-tuple-element.22), channel_id=1, source_target_pairs={{1,0},{2,1},{3,2},{4,3},{5,4},{6,5},{7,6},{9,8},{10,9},{11,10},{12... | collective-permute-start | bytes 18440 | tf_op jit(solution)/shard_map/ppermute | solution.py:24
  132.9 80.8 %collective-permute-start.6 = (f32[4,3,1,128]{3,2,1,0:T(1,128)}, f32[4,3,1,128]{3,2,1,0:T(1,128)S(1)}, u32[]{:S(2)}, u32[]{:S(2)}) collective-permute-start(f32[4,3,1,128]{3,2,1,0:T(1,128)} %get-tuple-element.23), channel_id=1, source_target_pairs={{0,1},{1,2},{2,3},{3,4},{4,5},{5,6},{6,7},{8,9},{9,10},{10,11},{11... | collective-permute-start | bytes 18440 | tf_op jit(solution)/shard_map/ppermute | solution.py:22
  139.0 74.7 %copy-start.4 = (s32[3,128,128]{2,1,0:T(8,128)S(1)}, s32[3,128,128]{2,1,0:T(8,128)}, u32[]{:S(2)}) copy-start(s32[3,128,128]{2,1,0:T(8,128)} %param.21) | copy-start | bytes 589828
  139.0 74.7 %copy-start.17 = (f32[128,128]{1,0:T(8,128)S(1)}, f32[128,128]{1,0:T(8,128)}, u32[]{:S(2)}) copy-start(f32[128,128]{1,0:T(8,128)} %copy-done.16) | copy-start | bytes 196612
  139.0 74.8 %copy-start.21 = (f32[128,128]{1,0:T(8,128)S(1)}, f32[128,128]{1,0:T(8,128)}, u32[]{:S(2)}) copy-start(f32[128,128]{1,0:T(8,128)} %get-tuple-element.43) | copy-start | bytes 196612
  139.0 74.7 %copy-start.41 = (f32[3,128,128]{2,1,0:T(8,128)S(1)}, f32[3,128,128]{2,1,0:T(8,128)}, u32[]{:S(2)}) copy-start(f32[3,128,128]{2,1,0:T(8,128)} %reduce-window_subtract_fusion.7) | copy-start | bytes 589828
  139.1 74.7 %copy-start.48 = (f32[128,128]{1,0:T(8,128)S(1)}, f32[128,128]{1,0:T(8,128)}, u32[]{:S(2)}) copy-start(f32[128,128]{1,0:T(8,128)} %get-tuple-element.44) | copy-start | bytes 196612
  213.7 1.6 copy-start.1
  213.7 1.6 copy-start.13
  213.7 1.6 copy-start.36
  213.7 1.6 copy-start.42
  213.7 1.6 copy-start.44
  216.8 12.7 %collective-permute-start.10 = (f32[2,3,128,1]{3,2,1,0:T(8,128)S(1)}, f32[2,3,128,1]{3,2,1,0:T(8,128)S(1)}, u32[]{:S(2)}, u32[]{:S(2)}) collective-permute-start(f32[2,3,128,1]{3,2,1,0:T(8,128)S(1)} %slice.630), channel_id=1, source_target_pairs={{504,0},{0,8},{8,16},{16,24},{24,32},{32,40},{40,48},{48,56},{56,6... | collective-permute-start | bytes 9224 | tf_op jit(solution)/shard_map/ppermute | solution.py:34
  219.1 10.4 %collective-permute-start.11 = (f32[2,3,1,128]{3,2,1,0:T(1,128)S(1)}, f32[2,3,1,128]{3,2,1,0:T(1,128)S(1)}, u32[]{:S(2)}, u32[]{:S(2)}) collective-permute-start(f32[2,3,1,128]{3,2,1,0:T(1,128)S(1)} %slice.632), channel_id=1, source_target_pairs={{0,1},{1,2},{2,3},{3,4},{4,5},{5,6},{6,7},{8,9},{9,10},{10,11},{11... | collective-permute-start | bytes 9224 | tf_op jit(solution)/shard_map/ppermute | solution.py:40
  231.1 11.5 %collective-permute-start.13 = (f32[4,3,128,1]{2,0,3,1:T(4,128)S(1)}, f32[4,3,128,1]{2,0,3,1:T(4,128)S(1)}, u32[]{:S(2)}, u32[]{:S(2)}) collective-permute-start(f32[4,3,128,1]{2,0,3,1:T(4,128)S(1)} %copy.506), channel_id=1, source_target_pairs={{8,0},{16,8},{24,16},{32,24},{40,32},{48,40},{56,48},{64,56},{72,6... | collective-permute-start | bytes 18440 | tf_op jit(solution)/shard_map/ppermute | solution.py:24
  233.3 9.6 %collective-permute-start.14 = (f32[4,3,128,1]{2,0,3,1:T(4,128)S(1)}, f32[4,3,128,1]{2,0,3,1:T(4,128)S(1)}, u32[]{:S(2)}, u32[]{:S(2)}) collective-permute-start(f32[4,3,128,1]{2,0,3,1:T(4,128)S(1)} %copy.508), channel_id=1, source_target_pairs={{0,8},{8,16},{16,24},{24,32},{32,40},{40,48},{48,56},{56,64},{64,7... | collective-permute-start | bytes 18440 | tf_op jit(solution)/shard_map/ppermute | solution.py:22
  235.8 81.6 %collective-permute-start.15 = (f32[4,3,1,128]{3,2,1,0:T(1,128)S(1)}, f32[4,3,1,128]{3,2,1,0:T(1,128)S(1)}, u32[]{:S(2)}, u32[]{:S(2)}) collective-permute-start(f32[4,3,1,128]{3,2,1,0:T(1,128)S(1)} %get-tuple-element.18), channel_id=1, source_target_pairs={{1,0},{2,1},{3,2},{4,3},{5,4},{6,5},{7,6},{9,8},{10,9},{11,10},{12... | collective-permute-start | bytes 18440 | tf_op jit(solution)/shard_map/ppermute | solution.py:24
  237.7 79.8 %collective-permute-start.12 = (f32[4,3,1,128]{3,2,1,0:T(1,128)S(1)}, f32[4,3,1,128]{3,2,1,0:T(1,128)S(1)}, u32[]{:S(2)}, u32[]{:S(2)}) collective-permute-start(f32[4,3,1,128]{3,2,1,0:T(1,128)S(1)} %get-tuple-element.19), channel_id=1, source_target_pairs={{0,1},{1,2},{2,3},{3,4},{4,5},{5,6},{6,7},{8,9},{9,10},{10,11},{11... | collective-permute-start | bytes 18440 | tf_op jit(solution)/shard_map/ppermute | solution.py:22
  317.5 1.6 copy-start.14
  317.5 1.6 copy-start.18
  317.5 1.6 copy-start.22
  317.5 1.6 copy-start.37
  320.4 12.9 %copy-start.33 = (f32[3,128,128]{2,1,0:T(8,128)S(1)}, f32[3,128,128]{2,1,0:T(8,128)}, u32[]{:S(2)}) copy-start(f32[3,128,128]{2,1,0:T(8,128)} %get-tuple-element.38) | copy-start | bytes 589828
  320.4 12.9 %copy-start.50 = (f32[128,128]{1,0:T(8,128)S(1)}, f32[128,128]{1,0:T(8,128)}, u32[]{:S(2)}) copy-start(f32[128,128]{1,0:T(8,128)} %get-tuple-element.41) | copy-start | bytes 196612
  320.6 12.7 %collective-permute-start.16 = (f32[2,3,128,1]{3,2,1,0:T(8,128)S(1)}, f32[2,3,128,1]{3,2,1,0:T(8,128)S(1)}, u32[]{:S(2)}, u32[]{:S(2)}) collective-permute-start(f32[2,3,128,1]{3,2,1,0:T(8,128)S(1)} %slice.649), channel_id=1, source_target_pairs={{504,0},{0,8},{8,16},{16,24},{24,32},{32,40},{40,48},{48,56},{56,6... | collective-permute-start | bytes 9224 | tf_op jit(solution)/shard_map/ppermute | solution.py:34
  323.1 10.3 %collective-permute-start.17 = (f32[2,3,1,128]{3,2,1,0:T(1,128)S(1)}, f32[2,3,1,128]{3,2,1,0:T(1,128)S(1)}, u32[]{:S(2)}, u32[]{:S(2)}) collective-permute-start(f32[2,3,1,128]{3,2,1,0:T(1,128)S(1)} %slice.651), channel_id=1, source_target_pairs={{0,1},{1,2},{2,3},{3,4},{4,5},{5,6},{6,7},{8,9},{9,10},{10,11},{11... | collective-permute-start | bytes 9224 | tf_op jit(solution)/shard_map/ppermute | solution.py:40
  335.0 12.0 %collective-permute-start.19 = (f32[4,3,128,1]{2,0,3,1:T(4,128)S(1)}, f32[4,3,128,1]{2,0,3,1:T(4,128)S(1)}, u32[]{:S(2)}, u32[]{:S(2)}) collective-permute-start(f32[4,3,128,1]{2,0,3,1:T(4,128)S(1)} %copy.515), channel_id=1, source_target_pairs={{8,0},{16,8},{24,16},{32,24},{40,32},{48,40},{56,48},{64,56},{72,6... | collective-permute-start | bytes 18440 | tf_op jit(solution)/shard_map/ppermute | solution.py:24
  337.2 10.2 %collective-permute-start.20 = (f32[4,3,128,1]{2,0,3,1:T(4,128)S(1)}, f32[4,3,128,1]{2,0,3,1:T(4,128)S(1)}, u32[]{:S(2)}, u32[]{:S(2)}) collective-permute-start(f32[4,3,128,1]{2,0,3,1:T(4,128)S(1)} %copy.517), channel_id=1, source_target_pairs={{0,8},{8,16},{16,24},{24,32},{32,40},{40,48},{48,56},{56,64},{64,7... | collective-permute-start | bytes 18440 | tf_op jit(solution)/shard_map/ppermute | solution.py:22
  340.3 83.0 %collective-permute-start.21 = (f32[4,3,1,128]{3,2,1,0:T(1,128)}, f32[4,3,1,128]{3,2,1,0:T(1,128)}, u32[]{:S(2)}, u32[]{:S(2)}) collective-permute-start(f32[4,3,1,128]{3,2,1,0:T(1,128)} %get-tuple-element.14), channel_id=1, source_target_pairs={{1,0},{2,1},{3,2},{4,3},{5,4},{6,5},{7,6},{9,8},{10,9},{11,10},{12... | collective-permute-start | bytes 18440 | tf_op jit(solution)/shard_map/ppermute | solution.py:24
  342.2 81.9 %collective-permute-start.18 = (f32[4,3,1,128]{3,2,1,0:T(1,128)}, f32[4,3,1,128]{3,2,1,0:T(1,128)}, u32[]{:S(2)}, u32[]{:S(2)}) collective-permute-start(f32[4,3,1,128]{3,2,1,0:T(1,128)} %get-tuple-element.15), channel_id=1, source_target_pairs={{0,1},{1,2},{2,3},{3,4},{4,5},{5,6},{6,7},{8,9},{9,10},{10,11},{11... | collective-permute-start | bytes 18440 | tf_op jit(solution)/shard_map/ppermute | solution.py:22
  348.1 76.0 %copy-start.5 = (s32[3,128,128]{2,1,0:T(8,128)S(1)}, s32[3,128,128]{2,1,0:T(8,128)}, u32[]{:S(2)}) copy-start(s32[3,128,128]{2,1,0:T(8,128)} %param.21) | copy-start | bytes 589828
  348.1 76.0 %copy-start.19 = (f32[128,128]{1,0:T(8,128)S(1)}, f32[128,128]{1,0:T(8,128)}, u32[]{:S(2)}) copy-start(f32[128,128]{1,0:T(8,128)} %copy-done.16) | copy-start | bytes 196612
  348.1 76.0 %copy-start.23 = (f32[128,128]{1,0:T(8,128)S(1)}, f32[128,128]{1,0:T(8,128)}, u32[]{:S(2)}) copy-start(f32[128,128]{1,0:T(8,128)} %get-tuple-element.43) | copy-start | bytes 196612
  421.7 2.4 copy-start.10
  424.1 2.2 copy-start.15
  424.1 2.2 copy-start.38
  424.1 2.2 copy-start.40
  424.1 2.2 copy-start.46
  426.3 2.1 copy-start.27
  426.3 2.1 copy-start.31
  428.7 12.9 %copy-start.34 = (f32[3,128,128]{2,1,0:T(8,128)S(1)}, f32[3,128,128]{2,1,0:T(8,128)}, u32[]{:S(2)}) copy-start(f32[3,128,128]{2,1,0:T(8,128)} %get-tuple-element.38) | copy-start | bytes 589828
  428.7 12.9 %copy-start.51 = (f32[128,128]{1,0:T(8,128)S(1)}, f32[128,128]{1,0:T(8,128)}, u32[]{:S(2)}) copy-start(f32[128,128]{1,0:T(8,128)} %get-tuple-element.41) | copy-start | bytes 196612
  428.9 12.7 %collective-permute-start.22 = (f32[2,3,128,1]{3,2,1,0:T(8,128)S(1)}, f32[2,3,128,1]{3,2,1,0:T(8,128)S(1)}, u32[]{:S(2)}, u32[]{:S(2)}) collective-permute-start(f32[2,3,128,1]{3,2,1,0:T(8,128)S(1)} %slice.668), channel_id=1, source_target_pairs={{504,0},{0,8},{8,16},{16,24},{24,32},{32,40},{40,48},{48,56},{56,6... | collective-permute-start | bytes 9224 | tf_op jit(solution)/shard_map/ppermute | solution.py:34
  431.1 10.4 %collective-permute-start.23 = (f32[2,3,1,128]{3,2,1,0:T(1,128)S(1)}, f32[2,3,1,128]{3,2,1,0:T(1,128)S(1)}, u32[]{:S(2)}, u32[]{:S(2)}) collective-permute-start(f32[2,3,1,128]{3,2,1,0:T(1,128)S(1)} %slice.670), channel_id=1, source_target_pairs={{0,1},{1,2},{2,3},{3,4},{4,5},{5,6},{6,7},{8,9},{9,10},{10,11},{11... | collective-permute-start | bytes 9224 | tf_op jit(solution)/shard_map/ppermute | solution.py:40
  (24 other events, 24.3 us)
where the time goes:
time: 444 us; the launch traced here: 443 us
  blocking collectives  295 us (66%)
  starting transfers between devices  75.5 us (17%)
  waiting for transfers between devices  29.7 us (7%)
  other arithmetic  24.7 us (6%)
  local copies, waits for them, and re-layouts  15.7 us (4%)
    all_gather x4, blocking collectives, fold_partner(): gathered = lax.all_gather(source_rows[None], 'zonal', axis=0, tiled=True)  295 us
    ppermute x4, waiting for transfers between devices, passed_along(): return lax.ppermute(block, axis, route)  29.7 us
    ppermute x8, starting transfers between devices, extended(): lax.ppermute(head, axis, [((i + 1) % count, i) for i in range(ends)])  27.9 us
    ppermute x8, starting transfers between devices, extended(): lax.ppermute(tail, axis, [(i, (i + 1) % count) for i in range(ends)])  26.6 us
    another operation x12, other arithmetic, water_column_weight(): return jnp.cumsum(gravity_density_term, axis=0) - 0.5 * gravity_density_term  14.2 us
    ppermute x4, starting transfers between devices, shifted(): return lax.ppermute(block, axis, route)  11.9 us
    ppermute x4, starting transfers between devices, passed_along(): return lax.ppermute(block, axis, route)  9.19 us
  transfers between devices with their start and end apart: 24, of which 4 were waited for; matrix products, arithmetic and copies ran while one was open for 3% of the time, Pallas kernels for 0%

commit v1 on v0

v1 whole, which is shorter than its diff:
```python
import jax
import jax.numpy as jnp
from jax import lax
from jax.experimental import pallas as pl
from jax.experimental.pallas import tpu as pltpu
from jax.sharding import PartitionSpec as P

STEPS = 4
LEVELS = 3
TIME_STEP = 0.25
VISCOSITY = 0.25
DIFFUSIVITY = 0.25

MESH = pl.DeviceIdType.MESH

N = 128
OFF = 16
ROWS = 160
CHUNK = 32
WIDE = 5
SLIM = 4
GROUP = 42
WEST_OWN = WIDE
EAST_FIRST = WIDE + 9
EAST_HALO = EAST_FIRST + 9
CA, CB, CC, CF, CGX, CGY, CHX, CHY, CDX, CDY, CK = range(11)
SIGN = (-1.0, -1.0, 1.0, 1.0)


def turned(x, shift):
    if isinstance(shift, int):
        shift %= N
        if shift == 0:
            return x
    return pltpu.roll(x, shift, 1)


def lanes(shape):
    return lax.broadcasted_iota(jnp.int32, shape, 1)


def coefficients(hx, hy, f):
    rx = 1.0 / hx
    ry = 1.0 / hy
    a = (TIME_STEP * VISCOSITY) * rx * rx
    b = (TIME_STEP * VISCOSITY) * ry * ry
    return (
        a,
        b,
        1.0 - 2.0 * (a + b),
        (0.5 * TIME_STEP) * f,
        TIME_STEP * rx,
        TIME_STEP * ry,
        0.5 * hx,
        0.5 * hy,
        DIFFUSIVITY * hy * rx,
        DIFFUSIVITY * hx * ry,
        TIME_STEP * rx * ry,
    )


def weights(t, s, lane):
    half = [0.25 * a - 0.2 * b for a, b in zip(t, s)]
    if len(half) == 1:
        one = jnp.where(lane >= GROUP, turned(half[0], GROUP), 0.0)
        two = jnp.where(lane >= 2 * GROUP, turned(half[0], 2 * GROUP), 0.0)
        return [half[0] + 2.0 * (one + two)]
    out = [half[0]]
    for k in range(1, LEVELS):
        out.append(out[-1] + (half[k - 1] + half[k]))
    return out


def advance(load, coef, masks, keep, east, west, rows, levels):
    lane = lanes((rows, N))
    span = range(levels)
    t = [load(2, k, 0) for k in span]
    s = [load(3, k, 0) for k in span]
    tn = [load(2, k, 1) for k in span]
    sn = [load(3, k, 1) for k in span]
    p = weights(t, s, lane)
    pn = weights(tn, sn, lane)
    for k in span:
        u, v = load(0, k, 0), load(1, k, 0)
        us, vs = load(0, k, -1), load(1, k, -1)
        uw = turned(u, west)
        mu, mv, mc = masks(k)
        un = mu * (
            coef(CC) * u
            + coef(CA) * (turned(u, east) + uw)
            + coef(CB) * (load(0, k, 1) + us)
            + coef(CF) * (v + vs)
            - coef(CGX) * (turned(p[k], east) - p[k])
        )
        vn = mv * (
            coef(CC) * v
            + coef(CA) * (turned(v, east) + turned(v, west))
            + coef(CB) * (load(1, k, 1) + vs)
            - coef(CF) * (u + uw)
            - coef(CGY) * (pn[k] - p[k])
        )
        keep(0, k, un)
        keep(1, k, vn)
        q, d = coef(CHY) * un, coef(CDX) * mu
        qp, qm = q + d, q - d
        r, e = coef(CHX) * vn, coef(CDY) * mv
        rp, rm = r + e, r - e
        scale = mc * coef(CK)
        for which, c, cn in ((2, t[k], tn[k]), (3, s[k], sn[k])):
            fe = qp * c + qm * turned(c, east)
            fn = rp * c + rm * cn
            below = keep(which + 2, k, fn)
            keep(which, k, c - scale * ((fe - turned(fe, west)) + (fn - below)))


def pack_wide(plane, rows):
    lane = lanes((rows, N))
    out = None
    for k in range(LEVELS):
        for g in range(8):
            first = GROUP * k + WIDE * g
            part = turned(plane(g, k), first - (N - WIDE))
            out = part if out is None else jnp.where(lane >= first, part, out)
    return out


def pack_slim(plane, rows):
    lane = lanes((rows, N))
    out = None
    for k in range(LEVELS):
        for g in range(8):
            first = GROUP * k + SLIM * g
            part = turned(plane(g, k), first)
            out = part if out is None else jnp.where(lane >= first, part, out)
    return out


def pack_own(plane, g, rows):
    lane = lanes((rows, N))
    out = None
    for k in range(LEVELS):
        x = plane(g, k)
        for first, column in ((GROUP * k + WEST_OWN, 0), (GROUP * k + EAST_FIRST, N - 9)):
            part = turned(x, first - column)
            out = part if out is None else jnp.where(lane >= first, part, out)
    return out


def merge_halo(own, wide, slim, g, rows):
    lane = lanes((rows, N))
    place = lane - jnp.where(lane >= 2 * GROUP, 2 * GROUP, jnp.where(lane >= GROUP, GROUP, 0))
    own = jnp.where(place < WIDE, turned(wide, -WIDE * g), own)
    east = (place >= EAST_HALO) & (place < EAST_HALO + SLIM)
    return jnp.where(east, turned(slim, EAST_HALO - SLIM * g), own)


def flipped(x):
    lane = lanes(x.shape)
    for bit in (64, 32, 16, 8, 4, 2, 1):
        if bit == 64:
            x = turned(x, 64)
        else:
            x = jnp.where((lane & bit) != 0, turned(x, bit), turned(x, -bit))
    return x


def kernel(
    hinge,
    u_ref,
    v_ref,
    t_ref,
    s_ref,
    hx_ref,
    hy_ref,
    f_ref,
    cell_ref,
    zonal_ref,
    merid_ref,
    u_out,
    v_out,
    t_out,
    s_out,
    main,
    edge,
    top_main,
    top_edge,
    flux_main,
    flux_edge,
    mask_main,
    mask_edge,
    mask_top_main,
    mask_top_edge,
    metric_main,
    metric_top,
    metric_edge,
    coef_main,
    coef_edge,
    coef_top_main,
    coef_top_edge,
    east_buf,
    west_buf,
    north_buf,
    south_buf,
    fold_tile,
    fold_west,
    fold_east,
    from_west,
    from_east,
    from_south,
    from_north,
    from_fold,
    from_corner,
    send_sem,
    recv_sem,
    local_sem,
):
    nz, nm = lax.axis_size("zonal"), lax.axis_size("merid")
    z, m = lax.axis_index("zonal"), lax.axis_index("merid")
    east_z, west_z = lax.rem(z + 1, nz), lax.rem(z + nz - 1, nz)
    fold_z = nz - 1 - z
    fold_up, fold_down = lax.rem(fold_z + 1, nz), lax.rem(fold_z + nz - 1, nz)
    top, bottom = m == nm - 1, m == 0
    inner = jnp.logical_not(top)
    raised = jnp.logical_not(bottom)

    def at(zz, mm):
        return {"zonal": zz, "merid": mm}

    barrier = pltpu.get_barrier_semaphore()

    def hail(zz, mm):
        pl.semaphore_signal(barrier, inc=1, device_id=at(zz, mm), device_id_type=MESH)

    hail(east_z, m)
    hail(west_z, m)

    @pl.when(raised)
    def _():
        for zz in (west_z, z, east_z):
            hail(zz, m - 1)

    @pl.when(inner)
    def _():
        for zz in (west_z, z, east_z):
            hail(zz, m + 1)

    @pl.when(top)
    def _():
        hail(fold_z, m)

        @pl.when(fold_up != z)
        def _():
            hail(fold_up, m)

        @pl.when(fold_down != z)
        def _():
            hail(fold_down, m)

    fields = (u_ref, v_ref, t_ref, s_ref)

    def fill(i, carry):
        here = pl.ds(pl.multiple_of(i * CHUNK, CHUNK), CHUNK)
        there = pl.ds(pl.multiple_of(OFF + i * CHUNK, 8), CHUNK)
        for k in range(LEVELS):
            mu = zonal_ref[k, here, :].astype(jnp.float32)
            mv = merid_ref[k, here, :].astype(jnp.float32)
            mc = cell_ref[k, here, :].astype(jnp.float32)
            mask_main[k, there, :] = mu
            mask_main[3 + k, there, :] = mv
            mask_main[6 + k, there, :] = mc
            for g, ref in enumerate(fields):
                main[0, 3 * g + k, there, :] = ref[k, here, :] * (mu, mv, mc, mc)[g]
        return carry

    lax.fori_loop(0, N // CHUNK, fill, 0)

    def plane_at(start, rows):
        def plane(g, k):
            if g < 4:
                return main[0, 3 * g + k, pl.ds(OFF + start, rows), :]
            if g == 4:
                return mask_main[6 + k, pl.ds(OFF + start, rows), :]
            return (hx_ref, hy_ref, f_ref)[g - 5][pl.ds(start, rows), :]

        return plane

    def number(g, k):
        return 3 * g + k if g < 5 else 15 + g - 5

    every = [(g, k) for g in range(5) for k in range(LEVELS)] + [(g, 0) for g in (5, 6, 7)]

    @pl.when(inner)
    def _():
        for g, k in every:
            i = number(g, k)
            north_buf[pl.ds(WIDE * i, WIDE), :] = plane_at(N - WIDE, WIDE)(g, k)

    @pl.when(top)
    def _():
        plane = plane_at(N - 8, 8)
        for g, k in every:
            i = number(g, k)
            tile = flipped(plane(g, k))
            fold_tile[i, :, :] = tile
            north_buf[pl.ds(WIDE * i, WIDE), :] = tile[8 - WIDE :, :]
            if g == 1:
                north_buf[pl.ds(90 + k, 1), :] = tile[2:3, :]

        def mirrored(g, k):
            return fold_tile[number(g, k)]

        fold_west[...] = pack_wide(mirrored, 8)
        fold_east[...] = pack_slim(mirrored, 8)

    def copy(src, dst, slot, zz, mm):
        return pltpu.make_async_remote_copy(
            src_ref=src,
            dst_ref=dst,
            send_sem=send_sem.at[slot],
            recv_sem=recv_sem.at[slot],
            device_id=at(zz, mm),
            device_id_type=MESH,
        )

    corner = lambda i: from_corner.at[i]
    low, high = pl.ds(0, 8), pl.ds(N - 8, 8)
    to_east = copy(east_buf, from_west, 0, east_z, m)
    to_west = copy(west_buf, from_east, 1, west_z, m)
    to_north = copy(north_buf, from_south, 2, z, m + 1)
    to_south = copy(south_buf, from_north, 3, z, m - 1)
    to_fold = copy(north_buf, from_fold, 4, fold_z, m)
    to_ne = copy(east_buf.at[high], corner(0), 5, east_z, m + 1)
    to_nw = copy(west_buf.at[high], corner(1), 6, west_z, m + 1)
    to_se = copy(east_buf.at[low], corner(2), 7, east_z, m - 1)
    to_sw = copy(west_buf.at[low], corner(3), 8, west_z, m - 1)
    to_fold_up = copy(fold_west, corner(2), 9, fold_up, m)
    to_fold_down = copy(fold_east, corner(3), 10, fold_down, m)
    keep_fold_up = pltpu.make_async_copy(fold_west, corner(2), local_sem.at[0])
    keep_fold_down = pltpu.make_async_copy(fold_east, corner(3), local_sem.at[1])

    same = jnp.where(fold_up == z, 1, 0) + jnp.where(fold_down == z, 1, 0)
    pl.semaphore_wait(barrier, 2 + jnp.where(bottom, 0, 3) + 3 - jnp.where(top, same, 0))

    @pl.when(top)
    def _():
        to_fold.start()

        @pl.when(fold_up != z)
        def _():
            to_fold_up.start()

        @pl.when(fold_up == z)
        def _():
            keep_fold_up.start()

        @pl.when(fold_down != z)
        def _():
            to_fold_down.start()

        @pl.when(fold_down == z)
        def _():
            keep_fold_down.start()

    @pl.when(inner)
    def _():
        to_north.start()

    def pack(i, carry):
        first = pl.multiple_of(i * CHUNK, CHUNK)
        plane = plane_at(first, CHUNK)
        east_buf[pl.ds(first, CHUNK), :] = pack_wide(plane, CHUNK)
        west_buf[pl.ds(first, CHUNK), :] = pack_slim(plane, CHUNK)
        return carry

    lax.fori_loop(0, N // CHUNK, pack, 0)
    to_east.start()
    to_west.start()

    @pl.when(inner)
    def _():
        to_ne.start()
        to_nw.start()

    for g, k in every:
        south_buf[pl.ds(SLIM * number(g, k), SLIM), :] = plane_at(0, SLIM)(g, k)

    @pl.when(raised)
    def _():
        to_south.start()
        to_se.start()
        to_sw.start()

    def prepare(i, carry):
        first = pl.multiple_of(i * CHUNK, CHUNK)
        here = pl.ds(first, CHUNK)
        there = pl.ds(pl.multiple_of(OFF + i * CHUNK, 8), CHUNK)
        for c, x in enumerate(coefficients(hx_ref[here, :], hy_ref[here, :], f_ref[here, :])):
            coef_main[c, there, :] = x
        plane = plane_at(first, CHUNK)
        for g in range(8):
            x = pack_own(plane, g, CHUNK)
            if g < 4:
                edge[0, g, there, :] = x
            elif g == 4:
                mask_edge[2, there, :] = x
            else:
                metric_edge[g - 5, there, :] = x
        return carry

    lax.fori_loop(0, N // CHUNK, prepare, 0)

    def step_rows(n, start, rows, state, flux, mask, coef, levels, align):
        def at_row(dj):
            first = OFF + start + dj
            if dj == 0 and align:
                first = pl.multiple_of(first, 8)
            return pl.ds(first, rows)

        def load(g, k, dj):
            return state[n, levels * g + k, at_row(dj), :]

        def keep(g, k, x):
            if g < 4:
                state[n + 1, levels * g + k, at_row(0), :] = x
                return None
            flux[n, levels * (g - 4) + k, at_row(0), :] = x
            return flux[n, levels * (g - 4) + k, at_row(-1), :]

        def masks(k):
            return [mask[levels * i + k, at_row(0), :] for i in range(3)]

        advance(load, lambda c: coef[c, at_row(0), :], masks, keep, N - 1, 1, rows, levels)

    def interior(n, carry):
        def chunk(i, inside):
            step_rows(n, i * CHUNK, CHUNK, main, flux_main, mask_main, coef_main, LEVELS, True)
            return inside

        return lax.fori_loop(0, N // CHUNK, chunk, carry)

    lax.fori_loop(0, STEPS, interior, 0)

    halo = pl.ds(OFF - 8, 8)

    @pl.when(raised)
    def _():
        to_north.wait_recv()
        to_ne.wait_recv()
        to_nw.wait_recv()
        last = pl.ds(OFF - WIDE, WIDE)
        for g, k in every:
            x = from_south[pl.ds(WIDE * number(g, k), WIDE), :]
            if g < 4:
                main[0, 3 * g + k, last, :] = x
            elif g == 4:
                mask_main[6 + k, last, :] = x
            else:
                metric_main[g - 5, pl.ds(8 - WIDE, WIDE), :] = x

    @pl.when(bottom)
    def _():
        zero = jnp.zeros((8, N), jnp.float32)
        for g, k in every:
            if g < 4:
                main[0, 3 * g + k, halo, :] = zero
            elif g == 4:
                mask_main[6 + k, halo, :] = zero
            else:
                metric_main[g - 5, :, :] = zero + 1.0
        for i in (0, 1):
            from_corner[i, :, :] = zero

    for k in range(LEVELS):
        mc = mask_main[6 + k, halo, :]
        mask_main[k, halo, :] = mc * turned(mc, N - 1)
        mask_main[3 + k, halo, :] = mc * mask_main[6 + k, pl.ds(OFF - 7, 8), :]
    for c, x in enumerate(coefficients(metric_main[0], metric_main[1], metric_main[2])):
        coef_main[c, halo, :] = x

    to_east.wait_recv()
    to_west.wait_recv()

    def edge_keep(g, rows, x, offset=0):
        if g < 4:
            edge[0, g, rows, :] = x
        elif g == 4:
            mask_edge[2, rows, :] = x
        else:
            metric_edge[g - 5, rows, :] = x

    def south_plane(g, k):
        if g < 4:
            return main[0, 3 * g + k, halo, :]
        if g == 4:
            return mask_main[6 + k, halo, :]
        return metric_main[g - 5, :, :]

    for g in range(8):
        x = pack_own(south_plane, g, 8)
        x = merge_halo(x, from_corner[0], from_corner[1], g, 8)
        if g in (5, 6):
            x = jnp.where(bottom, 1.0, x)
        edge_keep(g, halo, x)

    def unpack(i, carry):
        first = pl.multiple_of(i * CHUNK, CHUNK)
        there = pl.ds(pl.multiple_of(OFF + i * CHUNK, 8), CHUNK)
        wide = from_west[pl.ds(first, CHUNK), :]
        slim = from_east[pl.ds(first, CHUNK), :]
        for g in range(8):
            if g < 4:
                x = edge[0, g, there, :]
            elif g == 4:
                x = mask_edge[2, there, :]
            else:
                x = metric_edge[g - 5, there, :]
            edge_keep(g, there, merge_halo(x, wide, slim, g, CHUNK))
        return carry

    lax.fori_loop(0, N // CHUNK, unpack, 0)

    def edge_masks(start, rows):
        there = pl.ds(start, rows)
        mc = mask_edge[2, there, :]
        mask_edge[0, there, :] = mc * turned(mc, N - 1)
        mask_edge[1, there, :] = mc * mask_edge[2, pl.ds(start + 1, rows), :]

    def edge_ready(start, rows):
        there = pl.ds(start, rows)
        for c, x in enumerate(
            coefficients(metric_edge[0, there, :], metric_edge[1, there, :], metric_edge[2, there, :])
        ):
            coef_edge[c, there, :] = x

    edge_masks(OFF - 8, 8)
    edge_ready(OFF - 8, 8)

    def ready(i, carry):
        edge_masks(OFF + i * CHUNK, CHUNK)
        edge_ready(OFF + i * CHUNK, CHUNK)
        return carry

    lax.fori_loop(0, N // CHUNK, ready, 0)

    def south_side(n, carry):
        step_rows(n, n - WIDE, 8, main, flux_main, mask_main, coef_main, LEVELS, False)
        step_rows(n, -8, 8, edge, flux_edge, mask_edge, coef_edge, 1, True)

        def chunk(i, inside):
            step_rows(n, i * CHUNK, CHUNK, edge, flux_edge, mask_edge, coef_edge, 1, True)
            return inside

        return lax.fori_loop(0, N // CHUNK, chunk, carry)

    lax.fori_loop(0, STEPS, south_side, 0)

    strip = pl.ds(0, 8)
    for g, k in every:
        if g < 4:
            top_main[3 * g + k, strip, :] = jnp.zeros((8, N), jnp.float32)
        elif g == 4:
            mask_top_main[6 + k, strip, :] = jnp.zeros((8, N), jnp.float32)
        else:
            metric_top[g - 5, :, :] = jnp.ones((8, N), jnp.float32)

    def top_keep(g, k, first, x):
        rows = pl.ds(first, x.shape[0])
        if g < 4:
            top_main[3 * g + k, rows, :] = x
        elif g == 4:
            mask_top_main[6 + k, rows, :] = x
        else:
            metric_top[g - 5, pl.ds(first, x.shape[0]), :] = x

    @pl.when(inner)
    def _():
        to_south.wait_recv()
        to_se.wait_recv()
        to_sw.wait_recv()
        for g, k in every:
            top_keep(g, k, 0, from_north[pl.ds(SLIM * number(g, k), SLIM), :])

    @pl.when(top)
    def _():
        to_fold.wait_recv()

        @pl.when(fold_up != z)
        def _():
            to_fold_up.wait_recv()

        @pl.when(fold_up == z)
        def _():
            keep_fold_up.wait()

        @pl.when(fold_down != z)
        def _():
            to_fold_down.wait_recv()

        @pl.when(fold_down == z)
        def _():
            keep_fold_down.wait()

        for g, k in every:
            top_keep(g, k, 8 - WIDE, from_fold[pl.ds(WIDE * number(g, k), WIDE), :])
        for k in range(LEVELS):
            top_keep(1, k, 2, from_fold[pl.ds(90 + k, 1), :])

    east = jnp.where(top, 1, N - 1)
    west = jnp.where(top, N - 1, 1)

    def top_plane(g, k):
        if g < 4:
            return top_main[3 * g + k, strip, :]
        if g == 4:
            return mask_top_main[6 + k, strip, :]
        return metric_top[g - 5, :, :]

    edge_metric = []
    for g in range(8):
        x = merge_halo(pack_own(top_plane, g, 8), from_corner[2], from_corner[3], g, 8)
        if g < 4:
            top_edge[g, strip, :] = x
        elif g == 4:
            mask_top_edge[2, strip, :] = x
        else:
            edge_metric.append(x)
    for c, x in enumerate(coefficients(*edge_metric)):
        coef_top_edge[c, :, :] = x
    for c, x in enumerate(coefficients(metric_top[0], metric_top[1], metric_top[2])):
        coef_top_main[c, :, :] = x
    row = lax.broadcasted_iota(jnp.int32, (8, N), 0)
    mc = mask_edge[2, pl.ds(OFF + N - 8, 8), :]
    over = jnp.where(top, 1.0, pltpu.roll(mask_top_edge[2, strip, :], 7, 0))
    mask_edge[1, pl.ds(OFF + N - 8, 8), :] = mc * jnp.where(row == 7, over, pltpu.roll(mc, 7, 0))
    for mask, levels in ((mask_top_main, LEVELS), (mask_top_edge, 1)):
        for k in range(levels):
            mc = mask[2 * levels + k, strip, :]
            mask[k, strip, :] = mc * turned(mc, east)
            mask[levels + k, strip, :] = mc * jnp.where(row == 7, 1.0, pltpu.roll(mc, 7, 0))

    plain = [jnp.full((1, N), hinge[g], jnp.int32) == 0 for g in range(4)]

    first_row, last_row = row == 0, row == 7
    brim, under = pl.ds(OFF + N - 8, 8), pl.ds(OFF + N - 16, 8)

    def up(x):
        return pltpu.roll(x, 7, 0)

    def down(x):
        return pltpu.roll(x, 1, 0)

    kinds = (
        (LEVELS, main, flux_main, mask_main, mask_top_main, coef_main, coef_top_main),
        (1, edge, flux_edge, mask_edge, mask_top_edge, coef_edge, coef_top_edge),
    )

    def north_side(n, carry):
        after = []
        for (levels, state, flux, mask, mask_beyond, coef, coef_beyond), (below, beyond) in zip(
            kinds, carry
        ):
            new_below, new_beyond, fluxes = [None] * len(below), [None] * len(beyond), {}

            def load_below(g, k, dj):
                c, z = below[levels * g + k], beyond[levels * g + k]
                if dj == 0:
                    return c
                if dj < 0:
                    return jnp.where(first_row, down(state[n, levels * g + k, under, :]), down(c))
                ghost = SIGN[g] * jnp.where(plain[g], z, down(turned(z, 1)))
                return jnp.where(last_row, jnp.where(top, ghost, up(z)), up(c))

            def load_beyond(g, k, dj):
                c, z = below[levels * g + k], beyond[levels * g + k]
                if dj == 0:
                    return z
                if dj < 0:
                    return jnp.where(first_row, down(c), down(z))
                ghost = SIGN[g] * jnp.where(plain[g], c, down(turned(c, N - 1)))
                return jnp.where(last_row, ghost, up(z))

            def keep_below(g, k, x):
                if g < 4:
                    new_below[levels * g + k] = x
                    return None
                fluxes[g, k] = down(x)
                return jnp.where(
                    first_row, down(flux[n, levels * (g - 4) + k, under, :]), fluxes[g, k]
                )

            def keep_beyond(g, k, x):
                if g < 4:
                    new_beyond[levels * g + k] = x
                    return None
                return jnp.where(first_row, fluxes[g, k], down(x))

            def masks(k):
                return [mask[levels * i + k, brim, :] for i in range(3)]

            def masks_beyond(k):
                return [mask_beyond[levels * i + k, strip, :] for i in range(3)]

            advance(load_below, lambda c: coef[c, brim, :], masks, keep_below, N - 1, 1, 8, levels)
            advance(
                load_beyond, lambda c: coef_beyond[c], masks_beyond, keep_beyond, east, west, 8, levels
            )
            after.append((tuple(new_below), tuple(new_beyond)))
        return tuple(after)

    start = tuple(
        (
            tuple(state[0, i, brim, :] for i in range(4 * levels)),
            tuple(beyond[i, strip, :] for i in range(4 * levels)),
        )
        for levels, state, beyond in ((LEVELS, main, top_main), (1, edge, top_edge))
    )
    done = lax.fori_loop(0, STEPS, north_side, start)
    for state, (below, _) in zip((main, edge), done):
        for i, x in enumerate(below):
            state[STEPS, i, brim, :] = x

    def finish(i, carry):
        here = pl.ds(pl.multiple_of(i * CHUNK, CHUNK), CHUNK)
        there = pl.ds(pl.multiple_of(OFF + i * CHUNK, 8), CHUNK)
        lane = lanes((CHUNK, N))
        for g, ref in enumerate((u_out, v_out, t_out, s_out)):
            x = edge[STEPS, g, there, :]
            for k in range(LEVELS):
                y = main[STEPS, 3 * g + k, there, :]
                y = jnp.where(lane < WIDE, turned(x, -(GROUP * k + WEST_OWN)), y)
                sides = turned(x, N - SLIM - (GROUP * k + EAST_HALO - SLIM))
                ref[k, here, :] = jnp.where(lane >= N - SLIM, sides, y)
        return carry

    lax.fori_loop(0, N // CHUNK, finish, 0)

    to_east.wait_send()
    to_west.wait_send()

    @pl.when(inner)
    def _():
        for c in (to_north, to_ne, to_nw):
            c.wait_send()

    @pl.when(raised)
    def _():
        for c in (to_south, to_se, to_sw):
            c.wait_send()

    @pl.when(top)
    def _():
        to_fold.wait_send()

        @pl.when(fold_up != z)
        def _():
            to_fold_up.wait_send()

        @pl.when(fold_down != z)
        def _():
            to_fold_down.wait_send()


def per_device(u, v, t, s, hx, hy, f, cell, zonal, merid, hinge):
    def buf(*shape):
        return pltpu.VMEM(shape + (N,), jnp.float32)

    vmem = pl.BlockSpec(memory_space=pltpu.VMEM)
    shape = jax.ShapeDtypeStruct((LEVELS, N, N), jnp.float32)
    return pl.pallas_call(
        kernel,
        out_shape=(shape,) * 4,
        in_specs=[pl.BlockSpec(memory_space=pltpu.SMEM)] + [vmem] * 10,
        out_specs=(vmem,) * 4,
        scratch_shapes=[
            buf(5, 12, ROWS),
            buf(5, 4, ROWS),
            buf(12, 8),
            buf(4, 8),
            buf(4, 6, ROWS),
            buf(4, 2, ROWS),
            buf(9, ROWS),
            buf(3, ROWS),
            buf(9, 8),
            buf(3, 8),
            buf(3, 8),
            buf(3, 8),
            buf(3, ROWS),
            buf(11, ROWS),
            buf(11, ROWS),
            buf(11, 8),
            buf(11, 8),
            buf(N),
            buf(N),
            buf(96),
            buf(72),
            buf(18, 8),
            buf(8),
            buf(8),
            buf(N),
            buf(N),
            buf(96),
            buf(72),
            buf(96),
            buf(4, 8),
            pltpu.SemaphoreType.DMA((11,)),
            pltpu.SemaphoreType.DMA((11,)),
            pltpu.SemaphoreType.DMA((2,)),
        ],
        compiler_params=pltpu.CompilerParams(
            collective_id=0, has_side_effects=True, vmem_limit_bytes=48 * 1024 * 1024
        ),
        name="halo_steps",
    )(hinge, u, v, t, s, hx, hy, f, cell, zonal, merid)


def solution(mesh):
    field, plain = P(None, "merid", "zonal"), P("merid", "zonal")
    return jax.shard_map(
        per_device,
        mesh=mesh,
        in_specs=(field,) * 4 + (plain,) * 3 + (field,) * 3 + (P(),),
        out_specs=(field,) * 4,
        check_vma=False,
    )
```

time: 444 us -> 40.9 us (0.09)
  the two profiles are of different devices: /device:TPU:18 before, /device:TPU:26 now
where the time goes in v1:
time: 40.9 us; the launch traced here: 40.4 us
  Pallas kernels  27.4 us (67%)
  local copies, waits for them, and re-layouts  12.4 us (30%)
  between operations  0.66 us (2%)
    pallas_call x1, Pallas kernels, per_device(): pl.pallas_call(kernel, out_shape=(shape,) * 4, in_specs=[pl.BlockSpec(mem...  27.4 us
    unnamed x26, local copies, waits for them, and re-layouts  12.4 us

profile of v1, /device:TPU:26, one launch (start us, length us, event | category | flops | bytes accessed | tf_op | source)
XLA Modules:
  0.0 40.4 jit_solution(12603475773141977420)
XLA Ops:
  0.6 0.0 copy-start
  0.6 0.9 %copy-done = f32[3,128,128]{2,1,0:T(8,128)S(1)} copy-done((f32[3,128,128]{2,1,0:T(8,128)S(1)}, f32[3,128,128]{2,1,0:T(8,128)}, u32[]{:S(2)}) %copy-start) | copy-done | bytes 196632
  1.6 0.0 copy-start.1
  1.6 0.9 %copy-done.1 = f32[3,128,128]{2,1,0:T(8,128)S(1)} copy-done((f32[3,128,128]{2,1,0:T(8,128)S(1)}, f32[3,128,128]{2,1,0:T(8,128)}, u32[]{:S(2)}) %copy-start.1) | copy-done | bytes 196632
  2.5 0.0 copy-start.2
  2.5 0.9 %copy-done.2 = f32[3,128,128]{2,1,0:T(8,128)S(1)} copy-done((f32[3,128,128]{2,1,0:T(8,128)S(1)}, f32[3,128,128]{2,1,0:T(8,128)}, u32[]{:S(2)}) %copy-start.2) | copy-done | bytes 196632
  3.4 0.0 copy-start.3
  3.4 0.9 %copy-done.3 = f32[3,128,128]{2,1,0:T(8,128)S(1)} copy-done((f32[3,128,128]{2,1,0:T(8,128)S(1)}, f32[3,128,128]{2,1,0:T(8,128)}, u32[]{:S(2)}) %copy-start.3) | copy-done | bytes 196632
  4.3 0.0 copy-start.4
  4.3 0.9 %copy-done.4 = s32[3,128,128]{2,1,0:T(8,128)S(1)} copy-done((s32[3,128,128]{2,1,0:T(8,128)S(1)}, s32[3,128,128]{2,1,0:T(8,128)}, u32[]{:S(2)}) %copy-start.4) | copy-done | bytes 196632
  5.3 0.0 copy-start.5
  5.3 0.9 %copy-done.5 = s32[3,128,128]{2,1,0:T(8,128)S(1)} copy-done((s32[3,128,128]{2,1,0:T(8,128)S(1)}, s32[3,128,128]{2,1,0:T(8,128)}, u32[]{:S(2)}) %copy-start.5) | copy-done | bytes 196632
  6.2 0.0 copy-start.6
  6.2 0.9 %copy-done.6 = s32[3,128,128]{2,1,0:T(8,128)S(1)} copy-done((s32[3,128,128]{2,1,0:T(8,128)S(1)}, s32[3,128,128]{2,1,0:T(8,128)}, u32[]{:S(2)}) %copy-start.6) | copy-done | bytes 196632
  7.1 0.0 copy-start.7
  7.1 0.8 %copy-done.7 = f32[128,128]{1,0:T(8,128)S(1)} copy-done((f32[128,128]{1,0:T(8,128)S(1)}, f32[128,128]{1,0:T(8,128)}, u32[]{:S(2)}) %copy-start.7) | copy-done | bytes 65560
  8.0 0.0 copy-start.8
  8.0 0.8 %copy-done.8 = f32[128,128]{1,0:T(8,128)S(1)} copy-done((f32[128,128]{1,0:T(8,128)S(1)}, f32[128,128]{1,0:T(8,128)}, u32[]{:S(2)}) %copy-start.8) | copy-done | bytes 65560
  8.8 0.0 copy-start.9
  8.8 0.8 %copy-done.9 = f32[128,128]{1,0:T(8,128)S(1)} copy-done((f32[128,128]{1,0:T(8,128)S(1)}, f32[128,128]{1,0:T(8,128)}, u32[]{:S(2)}) %copy-start.9) | copy-done | bytes 65560
  9.6 0.0 copy-start.10
  9.6 0.7 %copy-done.10 = s32[4]{0:T(128)S(1)} copy-done((s32[4]{0:T(128)S(1)}, s32[4]{0:T(128)}, u32[]{:S(2)}) %copy-start.10) | copy-done | bytes 40
  10.3 27.4 %halo_steps.1 = (f32[3,128,128]{2,1,0:T(8,128)S(1)}, f32[3,128,128]{2,1,0:T(8,128)S(1)}, f32[3,128,128]{2,1,0:T(8,128)S(1)}, f32[3,128,128]{2,1,0:T(8,128)S(1)}) custom-call(s32[4]{0:T(128)S(1)} %copy-done.10, f32[3,128,128]{2,1,0:T(8,128)S(1)} %copy-done, f32[3,128,128]{2,1,0:T(8,128)S(1)} %copy-done.1, f32[3,128,128]{2,1,0:T(8,128)S(1)} %copy-done.2, ...), custom_call_target="tpu_custom_call" | custom-call | tf_op jit(solution)/shard_map/halo_steps/pallas_call | solution.py:769
  37.7 0.7 %copy.19 = f32[3,128,128]{2,1,0:T(8,128)} copy(f32[3,128,128]{2,1,0:T(8,128)S(1)} %get-tuple-element.8) | data formatting | bytes 393216
  38.4 0.7 %copy.20 = f32[3,128,128]{2,1,0:T(8,128)} copy(f32[3,128,128]{2,1,0:T(8,128)S(1)} %get-tuple-element.9) | data formatting | bytes 393216
  39.1 0.7 %copy.21 = f32[3,128,128]{2,1,0:T(8,128)} copy(f32[3,128,128]{2,1,0:T(8,128)S(1)} %get-tuple-element.10) | data formatting | bytes 393216
  39.8 0.7 %copy.22 = f32[3,128,128]{2,1,0:T(8,128)} copy(f32[3,128,128]{2,1,0:T(8,128)S(1)} %get-tuple-element.11) | data formatting | bytes 393216
Async XLA Ops:
  0.6 0.9 %copy-start = (f32[3,128,128]{2,1,0:T(8,128)S(1)}, f32[3,128,128]{2,1,0:T(8,128)}, u32[]{:S(2)}) copy-start(f32[3,128,128]{2,1,0:T(8,128)} %u_ref.1) | copy-start | bytes 589828
  1.6 0.9 %copy-start.1 = (f32[3,128,128]{2,1,0:T(8,128)S(1)}, f32[3,128,128]{2,1,0:T(8,128)}, u32[]{:S(2)}) copy-start(f32[3,128,128]{2,1,0:T(8,128)} %v_ref.1) | copy-start | bytes 589828
  2.5 0.9 %copy-start.2 = (f32[3,128,128]{2,1,0:T(8,128)S(1)}, f32[3,128,128]{2,1,0:T(8,128)}, u32[]{:S(2)}) copy-start(f32[3,128,128]{2,1,0:T(8,128)} %t_ref.1) | copy-start | bytes 589828
  3.4 0.9 %copy-start.3 = (f32[3,128,128]{2,1,0:T(8,128)S(1)}, f32[3,128,128]{2,1,0:T(8,128)}, u32[]{:S(2)}) copy-start(f32[3,128,128]{2,1,0:T(8,128)} %s_ref.1) | copy-start | bytes 589828
  4.3 0.9 %copy-start.4 = (s32[3,128,128]{2,1,0:T(8,128)S(1)}, s32[3,128,128]{2,1,0:T(8,128)}, u32[]{:S(2)}) copy-start(s32[3,128,128]{2,1,0:T(8,128)} %cell_ref.1) | copy-start | bytes 589828
  5.3 0.9 %copy-start.5 = (s32[3,128,128]{2,1,0:T(8,128)S(1)}, s32[3,128,128]{2,1,0:T(8,128)}, u32[]{:S(2)}) copy-start(s32[3,128,128]{2,1,0:T(8,128)} %zonal_ref.1) | copy-start | bytes 589828
  6.2 0.9 %copy-start.6 = (s32[3,128,128]{2,1,0:T(8,128)S(1)}, s32[3,128,128]{2,1,0:T(8,128)}, u32[]{:S(2)}) copy-start(s32[3,128,128]{2,1,0:T(8,128)} %merid_ref.1) | copy-start | bytes 589828
  7.1 0.8 %copy-start.7 = (f32[128,128]{1,0:T(8,128)S(1)}, f32[128,128]{1,0:T(8,128)}, u32[]{:S(2)}) copy-start(f32[128,128]{1,0:T(8,128)} %hx_ref.1) | copy-start | bytes 196612
  8.0 0.8 %copy-start.8 = (f32[128,128]{1,0:T(8,128)S(1)}, f32[128,128]{1,0:T(8,128)}, u32[]{:S(2)}) copy-start(f32[128,128]{1,0:T(8,128)} %hy_ref.1) | copy-start | bytes 196612
  8.8 0.8 %copy-start.9 = (f32[128,128]{1,0:T(8,128)S(1)}, f32[128,128]{1,0:T(8,128)}, u32[]{:S(2)}) copy-start(f32[128,128]{1,0:T(8,128)} %f_ref.1) | copy-start | bytes 196612
  9.6 0.7 %copy-start.10 = (s32[4]{0:T(128)S(1)}, s32[4]{0:T(128)}, u32[]{:S(2)}) copy-start(s32[4]{0:T(128)} %hinge.1) | copy-start | bytes 52

commit v2 on v1

--- a/solution.py
+++ b/solution.py
@@ -25,6 +25,15 @@
 EAST_HALO = EAST_FIRST + 9
 CA, CB, CC, CF, CGX, CGY, CHX, CHY, CDX, CDY, CK = range(11)
 SIGN = (-1.0, -1.0, 1.0, 1.0)
+
+
+def sweep(body, size):
+    def step(i, carry):
+        first = pl.multiple_of(i * size, 8)
+        body(first, pl.ds(first, size), pl.ds(pl.multiple_of(OFF + first, 8), size))
+        return carry
+
+    lax.fori_loop(0, N // size, step, 0)
 
 
 def turned(x, shift):
@@ -165,7 +174,21 @@
 
 
 def kernel(
-    hinge,
+    u_hbm,
+    v_hbm,
+    t_hbm,
+    s_hbm,
+    hx_hbm,
+    hy_hbm,
+    f_hbm,
+    cell_hbm,
+    zonal_hbm,
+    merid_hbm,
+    hinge_hbm,
+    u_out,
+    v_out,
+    t_out,
+    s_out,
     u_ref,
     v_ref,
     t_ref,
@@ -176,10 +199,7 @@
     cell_ref,
     zonal_ref,
     merid_ref,
-    u_out,
-    v_out,
-    t_out,
-    s_out,
+    hinge,
     main,
     edge,
     top_main,
@@ -213,7 +233,17 @@
     send_sem,
     recv_sem,
     local_sem,
+    load_sem,
 ):
+    sources = (u_hbm, v_hbm, t_hbm, s_hbm, cell_hbm, zonal_hbm, merid_hbm, hx_hbm, hy_hbm, f_hbm, hinge_hbm)
+    targets = (u_ref, v_ref, t_ref, s_ref, cell_ref, zonal_ref, merid_ref, hx_ref, hy_ref, f_ref, hinge)
+    loads = [
+        pltpu.make_async_copy(src, dst, load_sem.at[i])
+        for i, (src, dst) in enumerate(zip(sources, targets))
+    ]
+    for c in loads:
+        c.start()
+
     nz, nm = lax.axis_size("zonal"), lax.axis_size("merid")
     z, m = lax.axis_index("zonal"), lax.axis_index("merid")
     east_z, west_z = lax.rem(z + 1, nz), lax.rem(z + nz - 1, nz)
@@ -256,11 +286,11 @@
         def _():
             hail(fold_down, m)
 
+    for c in loads:
+        c.wait()
     fields = (u_ref, v_ref, t_ref, s_ref)
 
-    def fill(i, carry):
-        here = pl.ds(pl.multiple_of(i * CHUNK, CHUNK), CHUNK)
-        there = pl.ds(pl.multiple_of(OFF + i * CHUNK, 8), CHUNK)
+    def fill(first, here, there):
         for k in range(LEVELS):
             mu = zonal_ref[k, here, :].astype(jnp.float32)
             mv = merid_ref[k, here, :].astype(jnp.float32)
@@ -270,9 +300,8 @@
             mask_main[6 + k, there, :] = mc
             for g, ref in enumerate(fields):
                 main[0, 3 * g + k, there, :] = ref[k, here, :] * (mu, mv, mc, mc)[g]
-        return carry
-
-    lax.fori_loop(0, N // CHUNK, fill, 0)
+
+    sweep(fill, CHUNK)
 
     def plane_at(start, rows):
         def plane(g, k):
@@ -365,14 +394,12 @@
     def _():
         to_north.start()
 
-    def pack(i, carry):
-        first = pl.multiple_of(i * CHUNK, CHUNK)
+    def pack(first, here, there):
         plane = plane_at(first, CHUNK)
-        east_buf[pl.ds(first, CHUNK), :] = pack_wide(plane, CHUNK)
-        west_buf[pl.ds(first, CHUNK), :] = pack_slim(plane, CHUNK)
-        return carry
-
-    lax.fori_loop(0, N // CHUNK, pack, 0)
+        east_buf[here, :] = pack_wide(plane, CHUNK)
+        west_buf[here, :] = pack_slim(plane, CHUNK)
+
+    sweep(pack, CHUNK)
     to_east.start()
     to_west.start()
 
@@ -390,10 +417,7 @@
         to_se.start()
         to_sw.start()
 
-    def prepare(i, carry):
-        first = pl.multiple_of(i * CHUNK, CHUNK)
-        here = pl.ds(first, CHUNK)
-        there = pl.ds(pl.multiple_of(OFF + i * CHUNK, 8), CHUNK)
+    def prepare(first, here, there):
         for c, x in enumerate(coefficients(hx_ref[here, :], hy_ref[here, :], f_ref[here, :])):
             coef_main[c, there, :] = x
         plane = plane_at(first, CHUNK)
@@ -405,11 +429,10 @@
                 mask_edge[2, there, :] = x
             else:
                 metric_edge[g - 5, there, :] = x
-        return carry
-
-    lax.fori_loop(0, N // CHUNK, prepare, 0)
-
-    def step_rows(n, start, rows, state, flux, mask, coef, levels, align):
+
+    sweep(prepare, CHUNK)
+
+    def step_rows(n, start, rows, state, flux, mask, coef, levels, align=True):
         def at_row(dj):
             first = OFF + start + dj
             if dj == 0 and align:
@@ -433,7 +456,7 @@
 
     def interior(n, carry):
         def chunk(i, inside):
-            step_rows(n, i * CHUNK, CHUNK, main, flux_main, mask_main, coef_main, LEVELS, True)
+            step_rows(n, i * CHUNK, CHUNK, main, flux_main, mask_main, coef_main, LEVELS)
             return inside
 
         return lax.fori_loop(0, N // CHUNK, chunk, carry)
@@ -502,11 +525,9 @@
             x = jnp.where(bottom, 1.0, x)
         edge_keep(g, halo, x)
 
-    def unpack(i, carry):
-        first = pl.multiple_of(i * CHUNK, CHUNK)
-        there = pl.ds(pl.multiple_of(OFF + i * CHUNK, 8), CHUNK)
-        wide = from_west[pl.ds(first, CHUNK), :]
-        slim = from_east[pl.ds(first, CHUNK), :]
+    def unpack(first, here, there):
+        wide = from_west[here, :]
+        slim = from_east[here, :]
         for g in range(8):
             if g < 4:
                 x = edge[0, g, there, :]
@@ -515,9 +536,8 @@
             else:
                 x = metric_edge[g - 5, there, :]
             edge_keep(g, there, merge_halo(x, wide, slim, g, CHUNK))
-        return carry
-
-    lax.fori_loop(0, N // CHUNK, unpack, 0)
+
+    sweep(unpack, CHUNK)
 
     def edge_masks(start, rows):
         there = pl.ds(start, rows)
@@ -535,19 +555,18 @@
     edge_masks(OFF - 8, 8)
     edge_ready(OFF - 8, 8)
 
-    def ready(i, carry):
-        edge_masks(OFF + i * CHUNK, CHUNK)
-        edge_ready(OFF + i * CHUNK, CHUNK)
-        return carry
-
-    lax.fori_loop(0, N // CHUNK, ready, 0)
+    def ready(first, here, there):
+        edge_masks(OFF + first, CHUNK)
+        edge_ready(OFF + first, CHUNK)
+
+    sweep(ready, CHUNK)
 
     def south_side(n, carry):
         step_rows(n, n - WIDE, 8, main, flux_main, mask_main, coef_main, LEVELS, False)
-        step_rows(n, -8, 8, edge, flux_edge, mask_edge, coef_edge, 1, True)
+        step_rows(n, -8, 8, edge, flux_edge, mask_edge, coef_edge, 1)
 
         def chunk(i, inside):
-            step_rows(n, i * CHUNK, CHUNK, edge, flux_edge, mask_edge, coef_edge, 1, True)
+            step_rows(n, i * CHUNK, CHUNK, edge, flux_edge, mask_edge, coef_edge, 1)
             return inside
 
         return lax.fori_loop(0, N // CHUNK, chunk, carry)
@@ -719,9 +738,7 @@
         for i, x in enumerate(below):
             state[STEPS, i, brim, :] = x
 
-    def finish(i, carry):
-        here = pl.ds(pl.multiple_of(i * CHUNK, CHUNK), CHUNK)
-        there = pl.ds(pl.multiple_of(OFF + i * CHUNK, 8), CHUNK)
+    def finish(first, here, there):
         lane = lanes((CHUNK, N))
         for g, ref in enumerate((u_out, v_out, t_out, s_out)):
             x = edge[STEPS, g, there, :]
@@ -730,9 +747,8 @@
                 y = jnp.where(lane < WIDE, turned(x, -(GROUP * k + WEST_OWN)), y)
                 sides = turned(x, N - SLIM - (GROUP * k + EAST_HALO - SLIM))
                 ref[k, here, :] = jnp.where(lane >= N - SLIM, sides, y)
-        return carry
-
-    lax.fori_loop(0, N // CHUNK, finish, 0)
+
+    sweep(finish, CHUNK)
 
     to_east.wait_send()
     to_west.wait_send()
@@ -758,6 +774,11 @@
         @pl.when(fold_down != z)
         def _():
             to_fold_down.wait_send()
+
+
+def deliver(*refs):
+    for i in range(4):
+        refs[4 + i][...] = refs[i][...]
 
 
 def per_device(u, v, t, s, hx, hy, f, cell, zonal, merid, hinge):
@@ -766,12 +787,16 @@
 
     vmem = pl.BlockSpec(memory_space=pltpu.VMEM)
     shape = jax.ShapeDtypeStruct((LEVELS, N, N), jnp.float32)
-    return pl.pallas_call(
+    results = pl.pallas_call(
         kernel,
         out_shape=(shape,) * 4,
-        in_specs=[pl.BlockSpec(memory_space=pltpu.SMEM)] + [vmem] * 10,
+        in_specs=[pl.BlockSpec(memory_space=pltpu.HBM)] * 11,
         out_specs=(vmem,) * 4,
-        scratch_shapes=[
+        scratch_shapes=[buf(LEVELS, N)] * 4
+        + [buf(N)] * 3
+        + [pltpu.VMEM((LEVELS, N, N), jnp.int32)] * 3
+        + [pltpu.SMEM((4,), jnp.int32)]
+        + [
             buf(5, 12, ROWS),
             buf(5, 4, ROWS),
             buf(12, 8),
@@ -805,12 +830,22 @@
             pltpu.SemaphoreType.DMA((11,)),
             pltpu.SemaphoreType.DMA((11,)),
             pltpu.SemaphoreType.DMA((2,)),
+            pltpu.SemaphoreType.DMA((11,)),
         ],
         compiler_params=pltpu.CompilerParams(
-            collective_id=0, has_side_effects=True, vmem_limit_bytes=48 * 1024 * 1024
+            collective_id=0, has_side_effects=True, vmem_limit_bytes=60 * 1024 * 1024
         ),
         name="halo_steps",
-    )(hinge, u, v, t, s, hx, hy, f, cell, zonal, merid)
+    )(u, v, t, s, hx, hy, f, cell, zonal, merid, hinge)
+
+
+    return pl.pallas_call(
+        deliver,
+        out_shape=(shape,) * 4,
+        in_specs=[vmem] * 4,
+        out_specs=(vmem,) * 4,
+        name="deliver",
+    )(*results)
 
 
 def solution(mesh):

time: 40.9 us -> 31.7 us (0.78)
  local copies, waits for them, and re-layouts: 12.4 us -> 0 us
  Pallas kernels: 27.4 us -> 30.8 us
    unnamed x26 -> x0, local copies, waits for them, and re-layouts: 12.4 us -> none
    pallas_call x0 -> x1, Pallas kernels: none -> 2.11 us  [per_device(): pl.pallas_call(deliver, out_shape=(shape,) * 4, in_specs=[vmem] * 4, out_...]
    pallas_call x1, Pallas kernels: 27.4 us -> 28.7 us  [per_device(): pl.pallas_call(kernel, out_shape=(shape,) * 4, in_specs=[pl.BlockSpec(mem...]
where the time goes in v2:
time: 31.7 us; the launch traced here: 31.5 us
  Pallas kernels  30.8 us (97%)
  between operations  0.64 us (2%)
    pallas_call x1, Pallas kernels, per_device(): pl.pallas_call(kernel, out_shape=(shape,) * 4, in_specs=[pl.BlockSpec(mem...  28.7 us
    pallas_call x1, Pallas kernels, per_device(): pl.pallas_call(deliver, out_shape=(shape,) * 4, in_specs=[vmem] * 4, out_...  2.11 us

profile of v2, /device:TPU:26, one launch (start us, length us, event | category | flops | bytes accessed | tf_op | source)
XLA Modules:
  0.0 31.5 jit_solution(2881820394177903701)
XLA Ops:
  0.6 28.7 %halo_steps.1 = (f32[3,128,128]{2,1,0:T(8,128)}, f32[3,128,128]{2,1,0:T(8,128)}, f32[3,128,128]{2,1,0:T(8,128)}, f32[3,128,128]{2,1,0:T(8,128)}) custom-call(f32[3,128,128]{2,1,0:T(8,128)} %u_hbm.1, f32[3,128,128]{2,1,0:T(8,128)} %v_hbm.1, f32[3,128,128]{2,1,0:T(8,128)} %t_hbm.1, f32[3,128,128]{2,1,0:T(8,128)} %s_hbm.1, f32[128,128]{1,0:T(8,128)} %hx_hbm.1, ...), custom_call_target="tpu_custom_call" | custom-call | tf_op jit(solution)/shard_map/halo_steps/pallas_call | solution.py:790
  29.4 2.1 %deliver.1 = (f32[3,128,128]{2,1,0:T(8,128)}, f32[3,128,128]{2,1,0:T(8,128)}, f32[3,128,128]{2,1,0:T(8,128)}, f32[3,128,128]{2,1,0:T(8,128)}) custom-call(f32[3,128,128]{2,1,0:T(8,128)} %get-tuple-element.8.refs_0_, f32[3,128,128]{2,1,0:T(8,128)} %get-tuple-element.9.refs_1_, f32[3,128,128]{2,1,0:T(8,128)} %get-tuple-element.10.refs_2_, ...), custom_call_target="tpu_custom_call" | custom-call | tf_op jit(solution)/shard_map/deliver/pallas_call | solution.py:842

commit v3 on v2

--- a/solution.py
+++ b/solution.py
@@ -17,6 +17,10 @@
 OFF = 16
 ROWS = 160
 CHUNK = 32
+EDGE_ROWS = 128
+FILL = PACK = PREPARE = UNPACK = READY = FINISH = 128
+PARTS = 1
+PIECE = N // PARTS
 WIDE = 5
 SLIM = 4
 GROUP = 42
@@ -301,7 +305,7 @@
             for g, ref in enumerate(fields):
                 main[0, 3 * g + k, there, :] = ref[k, here, :] * (mu, mv, mc, mc)[g]
 
-    sweep(fill, CHUNK)
+    sweep(fill, FILL)
 
     def plane_at(start, rows):
         def plane(g, k):
@@ -353,8 +357,11 @@
 
     corner = lambda i: from_corner.at[i]
     low, high = pl.ds(0, 8), pl.ds(N - 8, 8)
-    to_east = copy(east_buf, from_west, 0, east_z, m)
-    to_west = copy(west_buf, from_east, 1, west_z, m)
+    to_east, to_west = [], []
+    for i in range(PARTS):
+        piece = pl.ds(i * PIECE, PIECE)
+        to_east.append(copy(east_buf.at[piece], from_west.at[piece], 11 + 2 * i, east_z, m))
+        to_west.append(copy(west_buf.at[piece], from_east.at[piece], 12 + 2 * i, west_z, m))
     to_north = copy(north_buf, from_south, 2, z, m + 1)
     to_south = copy(south_buf, from_north, 3, z, m - 1)
     to_fold = copy(north_buf, from_fold, 4, fold_z, m)
@@ -394,14 +401,12 @@
     def _():
         to_north.start()
 
-    def pack(first, here, there):
-        plane = plane_at(first, CHUNK)
-        east_buf[here, :] = pack_wide(plane, CHUNK)
-        west_buf[here, :] = pack_slim(plane, CHUNK)
-
-    sweep(pack, CHUNK)
-    to_east.start()
-    to_west.start()
+    for i in range(PARTS):
+        plane = plane_at(i * PIECE, PIECE)
+        east_buf[pl.ds(i * PIECE, PIECE), :] = pack_wide(plane, PIECE)
+        to_east[i].start()
+        west_buf[pl.ds(i * PIECE, PIECE), :] = pack_slim(plane, PIECE)
+        to_west[i].start()
 
     @pl.when(inner)
     def _():
@@ -420,9 +425,9 @@
     def prepare(first, here, there):
         for c, x in enumerate(coefficients(hx_ref[here, :], hy_ref[here, :], f_ref[here, :])):
             coef_main[c, there, :] = x
-        plane = plane_at(first, CHUNK)
+        plane = plane_at(first, PREPARE)
         for g in range(8):
-            x = pack_own(plane, g, CHUNK)
+            x = pack_own(plane, g, PREPARE)
             if g < 4:
                 edge[0, g, there, :] = x
             elif g == 4:
@@ -430,7 +435,7 @@
             else:
                 metric_edge[g - 5, there, :] = x
 
-    sweep(prepare, CHUNK)
+    sweep(prepare, PREPARE)
 
     def step_rows(n, start, rows, state, flux, mask, coef, levels, align=True):
         def at_row(dj):
@@ -500,8 +505,8 @@
     for c, x in enumerate(coefficients(metric_main[0], metric_main[1], metric_main[2])):
         coef_main[c, halo, :] = x
 
-    to_east.wait_recv()
-    to_west.wait_recv()
+    for c in to_east + to_west:
+        c.wait_recv()
 
     def edge_keep(g, rows, x, offset=0):
         if g < 4:
@@ -535,9 +540,9 @@
                 x = mask_edge[2, there, :]
             else:
                 x = metric_edge[g - 5, there, :]
-            edge_keep(g, there, merge_halo(x, wide, slim, g, CHUNK))
-
-    sweep(unpack, CHUNK)
+            edge_keep(g, there, merge_halo(x, wide, slim, g, UNPACK))
+
+    sweep(unpack, UNPACK)
 
     def edge_masks(start, rows):
         there = pl.ds(start, rows)
@@ -556,20 +561,20 @@
     edge_ready(OFF - 8, 8)
 
     def ready(first, here, there):
-        edge_masks(OFF + first, CHUNK)
-        edge_ready(OFF + first, CHUNK)
-
-    sweep(ready, CHUNK)
+        edge_masks(OFF + first, READY)
+        edge_ready(OFF + first, READY)
+
+    sweep(ready, READY)
 
     def south_side(n, carry):
         step_rows(n, n - WIDE, 8, main, flux_main, mask_main, coef_main, LEVELS, False)
         step_rows(n, -8, 8, edge, flux_edge, mask_edge, coef_edge, 1)
 
         def chunk(i, inside):
-            step_rows(n, i * CHUNK, CHUNK, edge, flux_edge, mask_edge, coef_edge, 1)
+            step_rows(n, i * EDGE_ROWS, EDGE_ROWS, edge, flux_edge, mask_edge, coef_edge, 1)
             return inside
 
-        return lax.fori_loop(0, N // CHUNK, chunk, carry)
+        return lax.fori_loop(0, N // EDGE_ROWS, chunk, carry)
 
     lax.fori_loop(0, STEPS, south_side, 0)
 
@@ -739,7 +744,7 @@
             state[STEPS, i, brim, :] = x
 
     def finish(first, here, there):
-        lane = lanes((CHUNK, N))
+        lane = lanes((FINISH, N))
         for g, ref in enumerate((u_out, v_out, t_out, s_out)):
             x = edge[STEPS, g, there, :]
             for k in range(LEVELS):
@@ -748,10 +753,10 @@
                 sides = turned(x, N - SLIM - (GROUP * k + EAST_HALO - SLIM))
                 ref[k, here, :] = jnp.where(lane >= N - SLIM, sides, y)
 
-    sweep(finish, CHUNK)
-
-    to_east.wait_send()
-    to_west.wait_send()
+    sweep(finish, FINISH)
+
+    for c in to_east + to_west:
+        c.wait_send()
 
     @pl.when(inner)
     def _():
@@ -777,8 +782,11 @@
 
 
 def deliver(*refs):
-    for i in range(4):
-        refs[4 + i][...] = refs[i][...]
+    copies = [pltpu.make_async_copy(refs[i], refs[4 + i], refs[8].at[i]) for i in range(4)]
+    for c in copies:
+        c.start()
+    for c in copies:
+        c.wait()
 
 
 def per_device(u, v, t, s, hx, hy, f, cell, zonal, merid, hinge):
@@ -789,7 +797,7 @@
     shape = jax.ShapeDtypeStruct((LEVELS, N, N), jnp.float32)
     results = pl.pallas_call(
         kernel,
-        out_shape=(shape,) * 4,
+        out_shape=(pltpu.VMEM((LEVELS, N, N), jnp.float32),) * 4,
         in_specs=[pl.BlockSpec(memory_space=pltpu.HBM)] * 11,
         out_specs=(vmem,) * 4,
         scratch_shapes=[buf(LEVELS, N)] * 4
@@ -827,8 +835,8 @@
             buf(72),
             buf(96),
             buf(4, 8),
-            pltpu.SemaphoreType.DMA((11,)),
-            pltpu.SemaphoreType.DMA((11,)),
+            pltpu.SemaphoreType.DMA((11 + 2 * PARTS,)),
+            pltpu.SemaphoreType.DMA((11 + 2 * PARTS,)),
             pltpu.SemaphoreType.DMA((2,)),
             pltpu.SemaphoreType.DMA((11,)),
         ],
@@ -843,9 +851,10 @@
         deliver,
         out_shape=(shape,) * 4,
         in_specs=[vmem] * 4,
-        out_specs=(vmem,) * 4,
+        out_specs=(pl.BlockSpec(memory_space=pl.ANY),) * 4,
+        scratch_shapes=[pltpu.SemaphoreType.DMA((4,))],
         name="deliver",
-    )(*results)
+    )(*(pltpu.with_memory_space_constraint(r, pltpu.VMEM) for r in results))
 
 
 def solution(mesh):

time: 31.7 us -> 25.8 us (0.81)
  Pallas kernels: 30.8 us -> 25 us
    pallas_call x1, Pallas kernels: 28.7 us -> 24.1 us  [per_device(): pl.pallas_call(kernel, out_shape=(pltpu.VMEM((LEVELS, N, N), jnp.float32)...]
    pallas_call x1, Pallas kernels: 2.11 us -> 0.91 us  [per_device(): pl.pallas_call(deliver, out_shape=(shape,) * 4, in_specs=[vmem] * 4, out_...]
where the time goes in v3:
time: 25.8 us; the launch traced here: 25.6 us
  Pallas kernels  25 us (97%)
  between operations  0.64 us (2%)
    pallas_call x1, Pallas kernels, per_device(): pl.pallas_call(kernel, out_shape=(pltpu.VMEM((LEVELS, N, N), jnp.float32)...  24.1 us
    pallas_call x1, Pallas kernels, per_device(): pl.pallas_call(deliver, out_shape=(shape,) * 4, in_specs=[vmem] * 4, out_...  0.91 us

profile of v3, /device:TPU:26, one launch (start us, length us, event | category | flops | bytes accessed | tf_op | source)
XLA Modules:
  0.0 25.6 jit_solution(205813784214436745)
XLA Ops:
  0.6 24.1 %halo_steps.1 = (f32[3,128,128]{2,1,0:T(8,128)S(1)}, f32[3,128,128]{2,1,0:T(8,128)S(1)}, f32[3,128,128]{2,1,0:T(8,128)S(1)}, f32[3,128,128]{2,1,0:T(8,128)S(1)}) custom-call(f32[3,128,128]{2,1,0:T(8,128)} %u_hbm.1, f32[3,128,128]{2,1,0:T(8,128)} %v_hbm.1, f32[3,128,128]{2,1,0:T(8,128)} %t_hbm.1, f32[3,128,128]{2,1,0:T(8,128)} %s_hbm.1, f32[128,128]{1,0:T(8,128)} %hx_hbm.1, ...), custom_call_target="tpu_custom_call" | custom-call | tf_op jit(solution)/shard_map/halo_steps/pallas_call | solution.py:798
  24.7 0.9 %deliver.1 = (f32[3,128,128]{2,1,0:T(8,128)}, f32[3,128,128]{2,1,0:T(8,128)}, f32[3,128,128]{2,1,0:T(8,128)}, f32[3,128,128]{2,1,0:T(8,128)}) custom-call(f32[3,128,128]{2,1,0:T(8,128)S(1)} %get-tuple-element.8.refs_0_, f32[3,128,128]{2,1,0:T(8,128)S(1)} %get-tuple-element.9.refs_1_, f32[3,128,128]{2,1,0:T(8,128)S(1)} %get-tuple-element.10.refs_2_, ...), custom_call_target="tpu_custom_call" | custom-call | tf_op jit(solution)/shard_map/deliver/pallas_call | solution.py:850

commit v4 on v3

--- a/solution.py
+++ b/solution.py
@@ -16,9 +16,8 @@
 N = 128
 OFF = 16
 ROWS = 160
-CHUNK = 32
-EDGE_ROWS = 128
-FILL = PACK = PREPARE = UNPACK = READY = FINISH = 128
+CHUNK = 128
+FILL = PACK = PREPARE = UNPACK = READY = 128
 PARTS = 1
 PIECE = N // PARTS
 WIDE = 5
@@ -93,6 +92,12 @@
     sn = [load(3, k, 1) for k in span]
     p = weights(t, s, lane)
     pn = weights(tn, sn, lane)
+    te = [turned(x, east) for x in t]
+    se = [turned(x, east) for x in s]
+    if levels == 1:
+        dp = [turned(p[0], east) - p[0]]
+    else:
+        dp = weights([a - b for a, b in zip(te, t)], [a - b for a, b in zip(se, s)], lane)
     for k in span:
         u, v = load(0, k, 0), load(1, k, 0)
         us, vs = load(0, k, -1), load(1, k, -1)
@@ -103,7 +108,7 @@
             + coef(CA) * (turned(u, east) + uw)
             + coef(CB) * (load(0, k, 1) + us)
             + coef(CF) * (v + vs)
-            - coef(CGX) * (turned(p[k], east) - p[k])
+            - coef(CGX) * dp[k]
         )
         vn = mv * (
             coef(CC) * v
@@ -119,8 +124,8 @@
         r, e = coef(CHX) * vn, coef(CDY) * mv
         rp, rm = r + e, r - e
         scale = mc * coef(CK)
-        for which, c, cn in ((2, t[k], tn[k]), (3, s[k], sn[k])):
-            fe = qp * c + qm * turned(c, east)
+        for which, c, ce, cn in ((2, t[k], te[k], tn[k]), (3, s[k], se[k], sn[k])):
+            fe = qp * c + qm * ce
             fn = rp * c + rm * cn
             below = keep(which + 2, k, fn)
             keep(which, k, c - scale * ((fe - turned(fe, west)) + (fn - below)))
@@ -189,10 +194,8 @@
     zonal_hbm,
     merid_hbm,
     hinge_hbm,
-    u_out,
-    v_out,
-    t_out,
-    s_out,
+    main_out,
+    edge_out,
     u_ref,
     v_ref,
     t_ref,
@@ -401,6 +404,13 @@
     def _():
         to_north.start()
 
+    for g, k in every:
+        south_buf[pl.ds(SLIM * number(g, k), SLIM), :] = plane_at(0, SLIM)(g, k)
+
+    @pl.when(raised)
+    def _():
+        to_south.start()
+
     for i in range(PARTS):
         plane = plane_at(i * PIECE, PIECE)
         east_buf[pl.ds(i * PIECE, PIECE), :] = pack_wide(plane, PIECE)
@@ -413,12 +423,8 @@
         to_ne.start()
         to_nw.start()
 
-    for g, k in every:
-        south_buf[pl.ds(SLIM * number(g, k), SLIM), :] = plane_at(0, SLIM)(g, k)
-
     @pl.when(raised)
     def _():
-        to_south.start()
         to_se.start()
         to_sw.start()
 
@@ -565,18 +571,6 @@
         edge_ready(OFF + first, READY)
 
     sweep(ready, READY)
-
-    def south_side(n, carry):
-        step_rows(n, n - WIDE, 8, main, flux_main, mask_main, coef_main, LEVELS, False)
-        step_rows(n, -8, 8, edge, flux_edge, mask_edge, coef_edge, 1)
-
-        def chunk(i, inside):
-            step_rows(n, i * EDGE_ROWS, EDGE_ROWS, edge, flux_edge, mask_edge, coef_edge, 1)
-            return inside
-
-        return lax.fori_loop(0, N // EDGE_ROWS, chunk, carry)
-
-    lax.fori_loop(0, STEPS, south_side, 0)
 
     strip = pl.ds(0, 8)
     for g, k in every:
@@ -678,7 +672,10 @@
         (1, edge, flux_edge, mask_edge, mask_top_edge, coef_edge, coef_top_edge),
     )
 
-    def north_side(n, carry):
+    def outer(n, carry):
+        step_rows(n, n - WIDE, 8, main, flux_main, mask_main, coef_main, LEVELS, False)
+        step_rows(n, -8, 8, edge, flux_edge, mask_edge, coef_edge, 1)
+        step_rows(n, 0, N - 8, edge, flux_edge, mask_edge, coef_edge, 1)
         after = []
         for (levels, state, flux, mask, mask_beyond, coef, coef_beyond), (below, beyond) in zip(
             kinds, carry
@@ -728,6 +725,9 @@
             advance(
                 load_beyond, lambda c: coef_beyond[c], masks_beyond, keep_beyond, east, west, 8, levels
             )
+            if levels == 1:
+                for i, x in enumerate(new_below):
+                    state[n + 1, i, brim, :] = x
             after.append((tuple(new_below), tuple(new_beyond)))
         return tuple(after)
 
@@ -738,22 +738,15 @@
         )
         for levels, state, beyond in ((LEVELS, main, top_main), (1, edge, top_edge))
     )
-    done = lax.fori_loop(0, STEPS, north_side, start)
-    for state, (below, _) in zip((main, edge), done):
-        for i, x in enumerate(below):
-            state[STEPS, i, brim, :] = x
-
-    def finish(first, here, there):
-        lane = lanes((FINISH, N))
-        for g, ref in enumerate((u_out, v_out, t_out, s_out)):
-            x = edge[STEPS, g, there, :]
-            for k in range(LEVELS):
-                y = main[STEPS, 3 * g + k, there, :]
-                y = jnp.where(lane < WIDE, turned(x, -(GROUP * k + WEST_OWN)), y)
-                sides = turned(x, N - SLIM - (GROUP * k + EAST_HALO - SLIM))
-                ref[k, here, :] = jnp.where(lane >= N - SLIM, sides, y)
-
-    sweep(finish, FINISH)
+    done = lax.fori_loop(0, STEPS, outer, start)
+    for i, x in enumerate(done[0][0]):
+        main[STEPS, i, brim, :] = x
+
+    inside = pl.ds(OFF, N)
+    for i in range(4 * LEVELS):
+        main_out[i, :, :] = main[STEPS, i, inside, :]
+    for i in range(4):
+        edge_out[i, :, :] = edge[STEPS, i, inside, :]
 
     for c in to_east + to_west:
         c.wait_send()
@@ -781,10 +774,19 @@
             to_fold_down.wait_send()
 
 
-def deliver(*refs):
-    copies = [pltpu.make_async_copy(refs[i], refs[4 + i], refs[8].at[i]) for i in range(4)]
-    for c in copies:
+def deliver(main_ref, edge_ref, u_out, v_out, t_out, s_out, held, sem):
+    lane = lanes((N, N))
+    copies = []
+    for g, out in enumerate((u_out, v_out, t_out, s_out)):
+        x = edge_ref[g]
+        for k in range(LEVELS):
+            y = main_ref[3 * g + k]
+            y = jnp.where(lane < WIDE, turned(x, -(GROUP * k + WEST_OWN)), y)
+            sides = turned(x, N - SLIM - (GROUP * k + EAST_HALO - SLIM))
+            held[3 * g + k, :, :] = jnp.where(lane >= N - SLIM, sides, y)
+        c = pltpu.make_async_copy(held.at[pl.ds(3 * g, LEVELS)], out, sem.at[g])
         c.start()
+        copies.append(c)
     for c in copies:
         c.wait()
 
@@ -797,9 +799,12 @@
     shape = jax.ShapeDtypeStruct((LEVELS, N, N), jnp.float32)
     results = pl.pallas_call(
         kernel,
-        out_shape=(pltpu.VMEM((LEVELS, N, N), jnp.float32),) * 4,
+        out_shape=(
+            pltpu.VMEM((4 * LEVELS, N, N), jnp.float32),
+            pltpu.VMEM((4, N, N), jnp.float32),
+        ),
         in_specs=[pl.BlockSpec(memory_space=pltpu.HBM)] * 11,
-        out_specs=(vmem,) * 4,
+        out_specs=(vmem,) * 2,
         scratch_shapes=[buf(LEVELS, N)] * 4
         + [buf(N)] * 3
         + [pltpu.VMEM((LEVELS, N, N), jnp.int32)] * 3
@@ -850,9 +855,9 @@
     return pl.pallas_call(
         deliver,
         out_shape=(shape,) * 4,
-        in_specs=[vmem] * 4,
+        in_specs=[vmem] * 2,
         out_specs=(pl.BlockSpec(memory_space=pl.ANY),) * 4,
-        scratch_shapes=[pltpu.SemaphoreType.DMA((4,))],
+        scratch_shapes=[buf(4 * LEVELS, N), pltpu.SemaphoreType.DMA((4,))],
         name="deliver",
     )(*(pltpu.with_memory_space_constraint(r, pltpu.VMEM) for r in results))
 

time: 25.8 us -> 25.5 us (0.988)
  the two profiles are of different devices: /device:TPU:26 before, /device:TPU:24 now
where the time goes in v4:
time: 25.5 us; the launch traced here: 25.4 us
  Pallas kernels  24.7 us (97%)
  between operations  0.64 us (3%)
    pallas_call x1, Pallas kernels, per_device(): pl.pallas_call(kernel, out_shape=(pltpu.VMEM((4 * LEVELS, N, N), jnp.floa...  23.6 us
    pallas_call x1, Pallas kernels, per_device(): pl.pallas_call(deliver, out_shape=(shape,) * 4, in_specs=[vmem] * 2, out_...  1.18 us

profile of v4, /device:TPU:24, one launch (start us, length us, event | category | flops | bytes accessed | tf_op | source)
XLA Modules:
  0.0 25.4 jit_solution(5968717619667965004)
XLA Ops:
  0.6 23.6 %halo_steps.1 = (f32[12,128,128]{2,1,0:T(8,128)S(1)}, f32[4,128,128]{2,1,0:T(8,128)S(1)}) custom-call(f32[3,128,128]{2,1,0:T(8,128)} %u_hbm.1, f32[3,128,128]{2,1,0:T(8,128)} %v_hbm.1, f32[3,128,128]{2,1,0:T(8,128)} %t_hbm.1, f32[3,128,128]{2,1,0:T(8,128)} %s_hbm.1, f32[128,128]{1,0:T(8,128)} %hx_hbm.1, f32[128,128]{1,0:T(8,128)} %hy_hbm.1, ...), custom_call_target="tpu_custom_call" | custom-call | tf_op jit(solution)/shard_map/halo_steps/pallas_call | solution.py:800
  24.2 1.2 %deliver.1 = (f32[3,128,128]{2,1,0:T(8,128)}, f32[3,128,128]{2,1,0:T(8,128)}, f32[3,128,128]{2,1,0:T(8,128)}, f32[3,128,128]{2,1,0:T(8,128)}) custom-call(f32[12,128,128]{2,1,0:T(8,128)S(1)} %get-tuple-element.6.main_ref, f32[4,128,128]{2,1,0:T(8,128)S(1)} %get-tuple-element.7.edge_ref), custom_call_target="tpu_custom_call" | custom-call | tf_op jit(solution)/shard_map/deliver/pallas_call | solution.py:855

commit v5 on v4

--- a/solution.py
+++ b/solution.py
@@ -479,8 +479,6 @@
     @pl.when(raised)
     def _():
         to_north.wait_recv()
-        to_ne.wait_recv()
-        to_nw.wait_recv()
         last = pl.ds(OFF - WIDE, WIDE)
         for g, k in every:
             x = from_south[pl.ds(WIDE * number(g, k), WIDE), :]
@@ -510,6 +508,168 @@
         mask_main[3 + k, halo, :] = mc * mask_main[6 + k, pl.ds(OFF - 7, 8), :]
     for c, x in enumerate(coefficients(metric_main[0], metric_main[1], metric_main[2])):
         coef_main[c, halo, :] = x
+
+    strip = pl.ds(0, 8)
+    for g, k in every:
+        if g < 4:
+            top_main[3 * g + k, strip, :] = jnp.zeros((8, N), jnp.float32)
+        elif g == 4:
+            mask_top_main[6 + k, strip, :] = jnp.zeros((8, N), jnp.float32)
+        else:
+            metric_top[g - 5, :, :] = jnp.ones((8, N), jnp.float32)
+
+    def top_keep(g, k, first, x):
+        rows = pl.ds(first, x.shape[0])
+        if g < 4:
+            top_main[3 * g + k, rows, :] = x
+        elif g == 4:
+            mask_top_main[6 + k, rows, :] = x
+        else:
+            metric_top[g - 5, pl.ds(first, x.shape[0]), :] = x
+
+    @pl.when(inner)
+    def _():
+        to_south.wait_recv()
+        for g, k in every:
+            top_keep(g, k, 0, from_north[pl.ds(SLIM * number(g, k), SLIM), :])
+
+    @pl.when(top)
+    def _():
+        to_fold.wait_recv()
+
+        for g, k in every:
+            top_keep(g, k, 8 - WIDE, from_fold[pl.ds(WIDE * number(g, k), WIDE), :])
+        for k in range(LEVELS):
+            top_keep(1, k, 2, from_fold[pl.ds(90 + k, 1), :])
+
+    east = jnp.where(top, 1, N - 1)
+    west = jnp.where(top, N - 1, 1)
+
+    def top_plane(g, k):
+        if g < 4:
+            return top_main[3 * g + k, strip, :]
+        if g == 4:
+            return mask_top_main[6 + k, strip, :]
+        return metric_top[g - 5, :, :]
+
+    for c, x in enumerate(coefficients(metric_top[0], metric_top[1], metric_top[2])):
+        coef_top_main[c, :, :] = x
+    row = lax.broadcasted_iota(jnp.int32, (8, N), 0)
+
+    def top_masks(mask, levels):
+        for k in range(levels):
+            mc = mask[2 * levels + k, strip, :]
+            mask[k, strip, :] = mc * turned(mc, east)
+            mask[levels + k, strip, :] = mc * jnp.where(row == 7, 1.0, pltpu.roll(mc, 7, 0))
+
+    top_masks(mask_top_main, LEVELS)
+
+    plain = [jnp.full((1, N), hinge[g], jnp.int32) == 0 for g in range(4)]
+
+    first_row, last_row = row == 0, row == 7
+    brim, under = pl.ds(OFF + N - 8, 8), pl.ds(OFF + N - 16, 8)
+
+    def up(x):
+        return pltpu.roll(x, 7, 0)
+
+    def down(x):
+        return pltpu.roll(x, 1, 0)
+
+    def north_side(n, carry, levels, state, flux, mask, mask_beyond, coef, coef_beyond):
+        below, beyond = carry
+        new_below, new_beyond, fluxes = [None] * len(below), [None] * len(beyond), {}
+
+        def load_below(g, k, dj):
+            c, z = below[levels * g + k], beyond[levels * g + k]
+            if dj == 0:
+                return c
+            if dj < 0:
+                return jnp.where(first_row, down(state[n, levels * g + k, under, :]), down(c))
+            ghost = SIGN[g] * jnp.where(plain[g], z, down(turned(z, 1)))
+            return jnp.where(last_row, jnp.where(top, ghost, up(z)), up(c))
+
+        def load_beyond(g, k, dj):
+            c, z = below[levels * g + k], beyond[levels * g + k]
+            if dj == 0:
+                return z
+            if dj < 0:
+                return jnp.where(first_row, down(c), down(z))
+            ghost = SIGN[g] * jnp.where(plain[g], c, down(turned(c, N - 1)))
+            return jnp.where(last_row, ghost, up(z))
+
+        def keep_below(g, k, x):
+            if g < 4:
+                new_below[levels * g + k] = x
+                return None
+            fluxes[g, k] = down(x)
+            return jnp.where(
+                first_row, down(flux[n, levels * (g - 4) + k, under, :]), fluxes[g, k]
+            )
+
+        def keep_beyond(g, k, x):
+            if g < 4:
+                new_beyond[levels * g + k] = x
+                return None
+            return jnp.where(first_row, fluxes[g, k], down(x))
+
+        def masks(k):
+            return [mask[levels * i + k, brim, :] for i in range(3)]
+
+        def masks_beyond(k):
+            return [mask_beyond[levels * i + k, strip, :] for i in range(3)]
+
+        advance(load_below, lambda c: coef[c, brim, :], masks, keep_below, N - 1, 1, 8, levels)
+        advance(
+            load_beyond, lambda c: coef_beyond[c], masks_beyond, keep_beyond, east, west, 8, levels
+        )
+        if levels == 1:
+            for i, x in enumerate(new_below):
+                state[n + 1, i, brim, :] = x
+        return tuple(new_below), tuple(new_beyond)
+
+    def main_sides(n, carry):
+        step_rows(n, n - WIDE, 8, main, flux_main, mask_main, coef_main, LEVELS, False)
+        return north_side(
+            n, carry, LEVELS, main, flux_main, mask_main, mask_top_main, coef_main, coef_top_main
+        )
+
+    def tiles(levels, state, beyond):
+        return (
+            tuple(state[0, i, brim, :] for i in range(4 * levels)),
+            tuple(beyond[i, strip, :] for i in range(4 * levels)),
+        )
+
+    below, _ = lax.fori_loop(0, STEPS, main_sides, tiles(LEVELS, main, top_main))
+    for i, x in enumerate(below):
+        main[STEPS, i, brim, :] = x
+
+    @pl.when(raised)
+    def _():
+        to_ne.wait_recv()
+        to_nw.wait_recv()
+
+    @pl.when(inner)
+    def _():
+        to_se.wait_recv()
+        to_sw.wait_recv()
+
+    @pl.when(top)
+    def _():
+        @pl.when(fold_up != z)
+        def _():
+            to_fold_up.wait_recv()
+
+        @pl.when(fold_up == z)
+        def _():
+            keep_fold_up.wait()
+
+        @pl.when(fold_down != z)
+        def _():
+            to_fold_down.wait_recv()
+
+        @pl.when(fold_down == z)
+        def _():
+            keep_fold_down.wait()
 
     for c in to_east + to_west:
         c.wait_recv()
@@ -572,67 +732,6 @@
 
     sweep(ready, READY)
 
-    strip = pl.ds(0, 8)
-    for g, k in every:
-        if g < 4:
-            top_main[3 * g + k, strip, :] = jnp.zeros((8, N), jnp.float32)
-        elif g == 4:
-            mask_top_main[6 + k, strip, :] = jnp.zeros((8, N), jnp.float32)
-        else:
-            metric_top[g - 5, :, :] = jnp.ones((8, N), jnp.float32)
-
-    def top_keep(g, k, first, x):
-        rows = pl.ds(first, x.shape[0])
-        if g < 4:
-            top_main[3 * g + k, rows, :] = x
-        elif g == 4:
-            mask_top_main[6 + k, rows, :] = x
-        else:
-            metric_top[g - 5, pl.ds(first, x.shape[0]), :] = x
-
-    @pl.when(inner)
-    def _():
-        to_south.wait_recv()
-        to_se.wait_recv()
-        to_sw.wait_recv()
-        for g, k in every:
-            top_keep(g, k, 0, from_north[pl.ds(SLIM * number(g, k), SLIM), :])
-
-    @pl.when(top)
-    def _():
-        to_fold.wait_recv()
-
-        @pl.when(fold_up != z)
-        def _():
-            to_fold_up.wait_recv()
-
-        @pl.when(fold_up == z)
-        def _():
-            keep_fold_up.wait()
-
-        @pl.when(fold_down != z)
-        def _():
-            to_fold_down.wait_recv()
-
-        @pl.when(fold_down == z)
-        def _():
-            keep_fold_down.wait()
-
-        for g, k in every:
-            top_keep(g, k, 8 - WIDE, from_fold[pl.ds(WIDE * number(g, k), WIDE), :])
-        for k in range(LEVELS):
-            top_keep(1, k, 2, from_fold[pl.ds(90 + k, 1), :])
-
-    east = jnp.where(top, 1, N - 1)
-    west = jnp.where(top, N - 1, 1)
-
-    def top_plane(g, k):
-        if g < 4:
-            return top_main[3 * g + k, strip, :]
-        if g == 4:
-            return mask_top_main[6 + k, strip, :]
-        return metric_top[g - 5, :, :]
-
     edge_metric = []
     for g in range(8):
         x = merge_halo(pack_own(top_plane, g, 8), from_corner[2], from_corner[3], g, 8)
@@ -644,103 +743,20 @@
             edge_metric.append(x)
     for c, x in enumerate(coefficients(*edge_metric)):
         coef_top_edge[c, :, :] = x
-    for c, x in enumerate(coefficients(metric_top[0], metric_top[1], metric_top[2])):
-        coef_top_main[c, :, :] = x
-    row = lax.broadcasted_iota(jnp.int32, (8, N), 0)
     mc = mask_edge[2, pl.ds(OFF + N - 8, 8), :]
     over = jnp.where(top, 1.0, pltpu.roll(mask_top_edge[2, strip, :], 7, 0))
     mask_edge[1, pl.ds(OFF + N - 8, 8), :] = mc * jnp.where(row == 7, over, pltpu.roll(mc, 7, 0))
-    for mask, levels in ((mask_top_main, LEVELS), (mask_top_edge, 1)):
-        for k in range(levels):
-            mc = mask[2 * levels + k, strip, :]
-            mask[k, strip, :] = mc * turned(mc, east)
-            mask[levels + k, strip, :] = mc * jnp.where(row == 7, 1.0, pltpu.roll(mc, 7, 0))
-
-    plain = [jnp.full((1, N), hinge[g], jnp.int32) == 0 for g in range(4)]
-
-    first_row, last_row = row == 0, row == 7
-    brim, under = pl.ds(OFF + N - 8, 8), pl.ds(OFF + N - 16, 8)
-
-    def up(x):
-        return pltpu.roll(x, 7, 0)
-
-    def down(x):
-        return pltpu.roll(x, 1, 0)
-
-    kinds = (
-        (LEVELS, main, flux_main, mask_main, mask_top_main, coef_main, coef_top_main),
-        (1, edge, flux_edge, mask_edge, mask_top_edge, coef_edge, coef_top_edge),
-    )
-
-    def outer(n, carry):
-        step_rows(n, n - WIDE, 8, main, flux_main, mask_main, coef_main, LEVELS, False)
+
+    top_masks(mask_top_edge, 1)
+
+    def edge_sides(n, carry):
         step_rows(n, -8, 8, edge, flux_edge, mask_edge, coef_edge, 1)
         step_rows(n, 0, N - 8, edge, flux_edge, mask_edge, coef_edge, 1)
-        after = []
-        for (levels, state, flux, mask, mask_beyond, coef, coef_beyond), (below, beyond) in zip(
-            kinds, carry
-        ):
-            new_below, new_beyond, fluxes = [None] * len(below), [None] * len(beyond), {}
-
-            def load_below(g, k, dj):
-                c, z = below[levels * g + k], beyond[levels * g + k]
-                if dj == 0:
-                    return c
-                if dj < 0:
-                    return jnp.where(first_row, down(state[n, levels * g + k, under, :]), down(c))
-                ghost = SIGN[g] * jnp.where(plain[g], z, down(turned(z, 1)))
-                return jnp.where(last_row, jnp.where(top, ghost, up(z)), up(c))
-
-            def load_beyond(g, k, dj):
-                c, z = below[levels * g + k], beyond[levels * g + k]
-                if dj == 0:
-                    return z
-                if dj < 0:
-                    return jnp.where(first_row, down(c), down(z))
-                ghost = SIGN[g] * jnp.where(plain[g], c, down(turned(c, N - 1)))
-                return jnp.where(last_row, ghost, up(z))
-
-            def keep_below(g, k, x):
-                if g < 4:
-                    new_below[levels * g + k] = x
-                    return None
-                fluxes[g, k] = down(x)
-                return jnp.where(
-                    first_row, down(flux[n, levels * (g - 4) + k, under, :]), fluxes[g, k]
-                )
-
-            def keep_beyond(g, k, x):
-                if g < 4:
-                    new_beyond[levels * g + k] = x
-                    return None
-                return jnp.where(first_row, fluxes[g, k], down(x))
-
-            def masks(k):
-                return [mask[levels * i + k, brim, :] for i in range(3)]
-
-            def masks_beyond(k):
-                return [mask_beyond[levels * i + k, strip, :] for i in range(3)]
-
-            advance(load_below, lambda c: coef[c, brim, :], masks, keep_below, N - 1, 1, 8, levels)
-            advance(
-                load_beyond, lambda c: coef_beyond[c], masks_beyond, keep_beyond, east, west, 8, levels
-            )
-            if levels == 1:
-                for i, x in enumerate(new_below):
-                    state[n + 1, i, brim, :] = x
-            after.append((tuple(new_below), tuple(new_beyond)))
-        return tuple(after)
-
-    start = tuple(
-        (
-            tuple(state[0, i, brim, :] for i in range(4 * levels)),
-            tuple(beyond[i, strip, :] for i in range(4 * levels)),
+        return north_side(
+            n, carry, 1, edge, flux_edge, mask_edge, mask_top_edge, coef_edge, coef_top_edge
         )
-        for levels, state, beyond in ((LEVELS, main, top_main), (1, edge, top_edge))
-    )
-    done = lax.fori_loop(0, STEPS, outer, start)
-    for i, x in enumerate(done[0][0]):
-        main[STEPS, i, brim, :] = x
+
+    lax.fori_loop(0, STEPS, edge_sides, tiles(1, edge, top_edge))
 
     inside = pl.ds(OFF, N)
     for i in range(4 * LEVELS):

time: 25.5 us -> 25.9 us (1.016)
  the two profiles are of different devices: /device:TPU:24 before, /device:TPU:27 now
where the time goes in v5:
time: 25.9 us; the launch traced here: 25.7 us
  Pallas kernels  25.1 us (97%)
  between operations  0.64 us (2%)
    pallas_call x1, Pallas kernels, per_device(): pl.pallas_call(kernel, out_shape=(pltpu.VMEM((4 * LEVELS, N, N), jnp.floa...  23.9 us
    pallas_call x1, Pallas kernels, per_device(): pl.pallas_call(deliver, out_shape=(shape,) * 4, in_specs=[vmem] * 2, out_...  1.18 us

profile of v5, /device:TPU:27, one launch (start us, length us, event | category | flops | bytes accessed | tf_op | source)
XLA Modules:
  0.0 25.7 jit_solution(245833760978562276)
XLA Ops:
  0.6 23.9 %halo_steps.1 = (f32[12,128,128]{2,1,0:T(8,128)S(1)}, f32[4,128,128]{2,1,0:T(8,128)S(1)}) custom-call(f32[3,128,128]{2,1,0:T(8,128)} %u_hbm.1, f32[3,128,128]{2,1,0:T(8,128)} %v_hbm.1, f32[3,128,128]{2,1,0:T(8,128)} %t_hbm.1, f32[3,128,128]{2,1,0:T(8,128)} %s_hbm.1, f32[128,128]{1,0:T(8,128)} %hx_hbm.1, f32[128,128]{1,0:T(8,128)} %hy_hbm.1, ...), custom_call_target="tpu_custom_call" | custom-call | tf_op jit(solution)/shard_map/halo_steps/pallas_call | solution.py:816
  24.5 1.2 %deliver.1 = (f32[3,128,128]{2,1,0:T(8,128)}, f32[3,128,128]{2,1,0:T(8,128)}, f32[3,128,128]{2,1,0:T(8,128)}, f32[3,128,128]{2,1,0:T(8,128)}) custom-call(f32[12,128,128]{2,1,0:T(8,128)S(1)} %get-tuple-element.6.main_ref, f32[4,128,128]{2,1,0:T(8,128)S(1)} %get-tuple-element.7.edge_ref), custom_call_target="tpu_custom_call" | custom-call | tf_op jit(solution)/shard_map/deliver/pallas_call | solution.py:871

commit v6 on v4

--- a/solution.py
+++ b/solution.py
@@ -173,13 +173,7 @@
 
 
 def flipped(x):
-    lane = lanes(x.shape)
-    for bit in (64, 32, 16, 8, 4, 2, 1):
-        if bit == 64:
-            x = turned(x, 64)
-        else:
-            x = jnp.where((lane & bit) != 0, turned(x, bit), turned(x, -bit))
-    return x
+    return jnp.take_along_axis(x, N - 1 - lanes(x.shape), axis=1)
 
 
 def kernel(

time: 25.5 us -> 25.1 us (0.984)
  Pallas kernels: 24.7 us -> 24.3 us
    pallas_call x1, Pallas kernels: 23.6 us -> 23.1 us  [per_device(): pl.pallas_call(kernel, out_shape=(pltpu.VMEM((4 * LEVELS, N, N), jnp.floa...]
where the time goes in v6:
time: 25.1 us; the launch traced here: 24.9 us
  Pallas kernels  24.3 us (97%)
  between operations  0.64 us (3%)
    pallas_call x1, Pallas kernels, per_device(): pl.pallas_call(kernel, out_shape=(pltpu.VMEM((4 * LEVELS, N, N), jnp.floa...  23.1 us
    pallas_call x1, Pallas kernels, per_device(): pl.pallas_call(deliver, out_shape=(shape,) * 4, in_specs=[vmem] * 2, out_...  1.18 us

profile of v6, /device:TPU:24, one launch (start us, length us, event | category | flops | bytes accessed | tf_op | source)
XLA Modules:
  0.0 24.9 jit_solution(18310578385038068598)
XLA Ops:
  0.6 23.1 %halo_steps.1 = (f32[12,128,128]{2,1,0:T(8,128)S(1)}, f32[4,128,128]{2,1,0:T(8,128)S(1)}) custom-call(f32[3,128,128]{2,1,0:T(8,128)} %u_hbm.1, f32[3,128,128]{2,1,0:T(8,128)} %v_hbm.1, f32[3,128,128]{2,1,0:T(8,128)} %t_hbm.1, f32[3,128,128]{2,1,0:T(8,128)} %s_hbm.1, f32[128,128]{1,0:T(8,128)} %hx_hbm.1, f32[128,128]{1,0:T(8,128)} %hy_hbm.1, ...), custom_call_target="tpu_custom_call" | custom-call | tf_op jit(solution)/shard_map/halo_steps/pallas_call | solution.py:794
  23.8 1.2 %deliver.1 = (f32[3,128,128]{2,1,0:T(8,128)}, f32[3,128,128]{2,1,0:T(8,128)}, f32[3,128,128]{2,1,0:T(8,128)}, f32[3,128,128]{2,1,0:T(8,128)}) custom-call(f32[12,128,128]{2,1,0:T(8,128)S(1)} %get-tuple-element.6.main_ref, f32[4,128,128]{2,1,0:T(8,128)S(1)} %get-tuple-element.7.edge_ref), custom_call_target="tpu_custom_call" | custom-call | tf_op jit(solution)/shard_map/deliver/pallas_call | solution.py:849

commit v7 on v6

--- a/solution.py
+++ b/solution.py
@@ -374,26 +374,6 @@
     same = jnp.where(fold_up == z, 1, 0) + jnp.where(fold_down == z, 1, 0)
     pl.semaphore_wait(barrier, 2 + jnp.where(bottom, 0, 3) + 3 - jnp.where(top, same, 0))
 
-    @pl.when(top)
-    def _():
-        to_fold.start()
-
-        @pl.when(fold_up != z)
-        def _():
-            to_fold_up.start()
-
-        @pl.when(fold_up == z)
-        def _():
-            keep_fold_up.start()
-
-        @pl.when(fold_down != z)
-        def _():
-            to_fold_down.start()
-
-        @pl.when(fold_down == z)
-        def _():
-            keep_fold_down.start()
-
     @pl.when(inner)
     def _():
         to_north.start()
@@ -421,6 +401,26 @@
     def _():
         to_se.start()
         to_sw.start()
+
+    @pl.when(top)
+    def _():
+        to_fold.start()
+
+        @pl.when(fold_up != z)
+        def _():
+            to_fold_up.start()
+
+        @pl.when(fold_up == z)
+        def _():
+            keep_fold_up.start()
+
+        @pl.when(fold_down != z)
+        def _():
+            to_fold_down.start()
+
+        @pl.when(fold_down == z)
+        def _():
+            keep_fold_down.start()
 
     def prepare(first, here, there):
         for c, x in enumerate(coefficients(hx_ref[here, :], hy_ref[here, :], f_ref[here, :])):

time: 25.1 us -> 24.9 us (level)
  the two profiles are of different devices: /device:TPU:24 before, /device:TPU:26 now
where the time goes in v7:
time: 24.9 us; the launch traced here: 24.8 us
  Pallas kernels  24.2 us (97%)
  between operations  0.64 us (3%)
    pallas_call x1, Pallas kernels, per_device(): pl.pallas_call(kernel, out_shape=(pltpu.VMEM((4 * LEVELS, N, N), jnp.floa...  23 us
    pallas_call x1, Pallas kernels, per_device(): pl.pallas_call(deliver, out_shape=(shape,) * 4, in_specs=[vmem] * 2, out_...  1.18 us

profile of v7, /device:TPU:26, one launch (start us, length us, event | category | flops | bytes accessed | tf_op | source)
XLA Modules:
  0.0 24.8 jit_solution(17675060534035170804)
XLA Ops:
  0.6 23.0 %halo_steps.1 = (f32[12,128,128]{2,1,0:T(8,128)S(1)}, f32[4,128,128]{2,1,0:T(8,128)S(1)}) custom-call(f32[3,128,128]{2,1,0:T(8,128)} %u_hbm.1, f32[3,128,128]{2,1,0:T(8,128)} %v_hbm.1, f32[3,128,128]{2,1,0:T(8,128)} %t_hbm.1, f32[3,128,128]{2,1,0:T(8,128)} %s_hbm.1, f32[128,128]{1,0:T(8,128)} %hx_hbm.1, f32[128,128]{1,0:T(8,128)} %hy_hbm.1, ...), custom_call_target="tpu_custom_call" | custom-call | tf_op jit(solution)/shard_map/halo_steps/pallas_call | solution.py:794
  23.6 1.2 %deliver.1 = (f32[3,128,128]{2,1,0:T(8,128)}, f32[3,128,128]{2,1,0:T(8,128)}, f32[3,128,128]{2,1,0:T(8,128)}, f32[3,128,128]{2,1,0:T(8,128)}) custom-call(f32[12,128,128]{2,1,0:T(8,128)S(1)} %get-tuple-element.6.main_ref, f32[4,128,128]{2,1,0:T(8,128)S(1)} %get-tuple-element.7.edge_ref), custom_call_target="tpu_custom_call" | custom-call | tf_op jit(solution)/shard_map/deliver/pallas_call | solution.py:849
